TPU v7x, 256 devices: a whole 4x4x8 slice. The times are simulated.
256 devices in a mesh: ang: 32 (over y, z), rad: 8 (over x, core).
Axes of the slice: x: 4, y: 4, z: 8, core: 2. Of those that a mesh axis runs over, the one named last changes fastest.
Arguments:
- grid_field: bfloat16 [2, 128, 768, 1536], P(None, 'rad', 'ang'), may hold values from -6 to 6
- slot_order: int32 [512], replicated, may hold values from 0 to 511, as said below
- legendre: bfloat16 [512, 384, 512], P('ang'), may hold values from -0.21875 to 0.21875
- inverses: bfloat16 [512, 128, 128], P('rad'), may hold values from -0.2 to 1.7, as said below
Outputs:
- spectrum: float32 [2, 512, 2, 512, 128], P(None, 'ang', None, 'rad')
Inputs may be any that keep to these rules, and one draw needn't show every extreme that they name: `slot_order`: slots 2 k and 2 k + 1 hold orders m and 511 - m; every order appears in exactly one slot. `inverses`: each degree's matrix is a diagonal part between 0.5 and 1.5 plus entries of zero mean and magnitude at most 0.19.
All inputs are finite; a program needn't handle non-finite values.
Results may differ from a plain program's by a relative error of at most 0.0057.
Values may be sent and summed in bfloat16 or wider, within the bound.
No kernel may reach another device: no remote copies, remote signals or barrier semaphores. Data moves between devices by JAX's collectives and lax.ppermute only.
A program may use at most 128 MiB of HBM per device.

v0:
```python
import math

import jax
import jax.numpy as jnp
from jax import lax
from jax.sharding import PartitionSpec as P

LONS = 1536


def fourier_rows(slot_order):
    longitude = jnp.arange(LONS, dtype=jnp.int32)
    phase = slot_order[:, None] * longitude[None, :] % LONS
    angle = phase.astype(jnp.float32) * (2.0 * math.pi / LONS)
    factor = 1.0 / math.sqrt(LONS)
    stacked = jnp.stack([jnp.cos(angle) * factor, -jnp.sin(angle) * factor], axis=1)
    return stacked.astype(jnp.bfloat16)


def legendre_dense(symmetric, antisymmetric, legendre, orders_here):
    even_part = jnp.einsum(
        "shl,skfrh->slkfr", legendre, symmetric, preferred_element_type=jnp.float32
    )
    odd_part = jnp.einsum(
        "shl,skfrh->slkfr", legendre, antisymmetric, preferred_element_type=jnp.float32
    )
    degree = jnp.arange(legendre.shape[2], dtype=jnp.int32)
    parity = ((degree[None, :] + orders_here[:, None]) % 2 == 0)[:, :, None, None, None]
    keeping = (degree[None, :] >= orders_here[:, None])[:, :, None, None, None]
    chosen = jnp.where(parity, even_part, odd_part)
    return jnp.where(keeping, chosen, jnp.zeros_like(chosen)).astype(jnp.bfloat16)


def solve_block(received, orders_here, legendre, inverses):
    half = received.shape[-1] // 2
    northern = received[..., :half].astype(jnp.float32)
    southern = received[..., half:][..., ::-1].astype(jnp.float32)
    symmetric = (northern + southern).astype(jnp.bfloat16)
    antisymmetric = (northern - southern).astype(jnp.bfloat16)
    coefficients = legendre_dense(symmetric, antisymmetric, legendre, orders_here)
    moved = lax.all_to_all(coefficients, "rad", split_axis=1, concat_axis=4, tiled=True)
    return jnp.einsum("slkfr,lqr->ksflq", moved, inverses, preferred_element_type=jnp.float32)


def body(grid_field, slot_order, legendre, inverses):
    fourier_table = fourier_rows(slot_order)
    fourier = jnp.einsum(
        "skj,frij->skfri", fourier_table, grid_field, preferred_element_type=jnp.float32
    ).astype(jnp.bfloat16)
    slots_here = legendre.shape[0]
    orders_here = lax.dynamic_slice_in_dim(
        slot_order, lax.axis_index("ang") * slots_here, slots_here
    )
    received = lax.all_to_all(fourier, "ang", split_axis=0, concat_axis=4, tiled=True)
    return solve_block(received, orders_here, legendre, inverses)


def solution(mesh):
    placed = (P(None, "rad", "ang", None), P(), P("ang", None, None), P("rad", None, None))
    return jax.shard_map(
        body,
        mesh=mesh,
        in_specs=placed,
        out_specs=P(None, "ang", None, "rad", None),
        check_vma=False,
    )
```

profile of v0, /device:TPU:1, one launch (start us, length us, event | category | flops | bytes accessed | tf_op | source)
XLA Modules:
  0.0 227.8 jit_solution(629943484964595453)
XLA Ops:
  0.0 0.0 copy-start
  0.0 14.6 %multiply_convert_fusion.1 = (bf16[512,1,1536]{2,0,1:T(8,128)(2,1)S(1)}, bf16[512,1,1536]{2,0,1:T(8,128)(2,1)S(1)}) fusion(s32[512]{0:T(512)} %param.5), kind=kLoop, calls=%fused_computation.12 | loop fusion | flops 11010048 | bytes 3147776 | tf_op jit(solution)/shard_map/convert
  14.6 0.0 copy-done
  14.6 4.0 %fusion.15 = bf16[512,2,2,16,24]{0,4,3,2,1:T(8,128)(2,1)} fusion(bf16[2,16,24,1536]{3,2,1,0:T(8,128)(2,1)S(1)} %copy-done, bf16[512,1,1536]{2,0,1:T(8,128)(2,1)S(1)} %get-tuple-element.6, bf16[512,1,1536]{2,0,1:T(8,128)(2,1)S(1)} %get-tuple-element.5), kind=kOutput, calls=%fused_computation.23 | convolution fusion | flops 2422996992 | bytes 7077888 | tf_op jit(solution)/shard_map/skj,frij->skfri/dot_general | solution.py:47
  18.6 12.7 %copy.12 = bf16[512,2,2,16,24]{4,3,2,1,0:T(8,128)(2,1)} copy(bf16[512,2,2,16,24]{0,4,3,2,1:T(8,128)(2,1)} %fusion.15) | data formatting | bytes 3145728 | tf_op jit(solution)/shard_map/convert_element_type | solution.py:49
  31.3 12.7 %reshape.141 = bf16[32,2,12288]{2,1,0:T(2,128)(2,1)} reshape(bf16[512,2,2,16,24]{4,3,2,1,0:T(8,128)(2,1)} %copy.12) | data formatting | bytes 3145728
  44.0 12.0 %all-to-all-start = ((bf16[32,2,12288]{2,1,0:T(2,128)(2,1)}), bf16[32,2,12288]{2,1,0:T(2,128)(2,1)S(1)}, u32[]{:S(2)}, u32[]{:S(2)}) async-start(bf16[32,2,12288]{2,1,0:T(2,128)(2,1)} %reshape.141), calls=%async_computation | async-start | bytes 3145728 | tf_op jit(solution)/shard_map/all_to_all | solution.py:54
  56.0 0.8 dynamic_slice.3
  56.8 0.1 iota_compare_fusion
  56.9 35.9 %all-to-all-done = bf16[32,2,12288]{2,1,0:T(2,128)(2,1)S(1)} async-done(((bf16[32,2,12288]{2,1,0:T(2,128)(2,1)}), bf16[32,2,12288]{2,1,0:T(2,128)(2,1)S(1)}, u32[]{:S(2)}, u32[]{:S(2)}) %all-to-all-start) | async-done | bytes 1572896 | tf_op jit(solution)/shard_map/all_to_all | solution.py:54
  92.8 12.8 %reshape.142 = bf16[512,2,2,16,24]{4,3,2,1,0:T(8,128)(2,1)} reshape(bf16[32,2,12288]{2,1,0:T(2,128)(2,1)S(1)} %all-to-all-done) | data formatting | bytes 3145728
  105.7 20.0 %copy.14 = bf16[16,2,2,16,32,24]{5,4,3,2,1,0:T(8,128)(2,1)} copy(bf16[16,2,2,16,32,24]{5,3,2,1,0,4:T(8,128)(2,1)} %bitcast.49) | data formatting | bytes 3145728 | tf_op jit(solution)/shard_map/all_to_all | solution.py:54
  125.7 12.2 %all_to_all.29 = bf16[16,2,2,16,768]{4,3,2,1,0:T(8,128)(2,1)S(1)} reshape(bf16[16,2,2,16,32,24]{5,4,3,2,1,0:T(8,128)(2,1)} %copy.14) | data formatting | bytes 3145728 | tf_op jit(solution)/shard_map/all_to_all | solution.py:54
  137.9 0.1 slice.9
  138.0 0.7 rev.3
  138.7 4.0 %fusion = bf16[16,2,2,16,512]{4,3,2,1,0:T(8,128)(2,1)S(1)} fusion(bf16[16,384,512]{2,1,0:T(8,128)(2,1)} %param.6, bf16[16,2,2,16,384]{4,3,2,1,0:T(8,128)(2,1)S(1)} %rev.3, bf16[16,2,2,16,768]{4,3,2,1,0:T(8,128)(2,1)S(1)} %all_to_all.29), kind=kOutput, calls=%fused_computation | convolution fusion | flops 404226048 | bytes 8912896 | tf_op jit(solution)/shard_map/shl,skfrh->slkfr/dot_general | solution.py:24
  142.7 4.0 %fusion.25 = bf16[16,512,2,2,16]{1,4,3,2,0:T(8,128)(2,1)S(1)} fusion(bf16[16,2,2,16,512]{4,3,2,1,0:T(8,128)(2,1)S(1)} %fusion, bf16[16,384,512]{2,1,0:T(8,128)(2,1)} %param.6, pred[16,512]{1,0:T(8,128)(4,1)S(1)} %get-tuple-element.8, pred[16,512]{1,0:T(8,128)(4,1)S(1)} %get-tuple-element.7, bf16[16,2,2,16,384]{4,3,2,1,0:T(8,128)(2,1)S(1)} %rev.3, ...), kind=kOutput, calls=%fused_computation.27 | convolution fusion | flops 405274624 | bytes 9977856 | tf_op jit(solution)/shard_map/shl,skfrh->slkfr/dot_general | solution.py:21
  146.7 14.8 %copy.15 = bf16[16,512,2,2,16]{4,3,2,0,1:T(2,128)(2,1)} copy(bf16[16,512,2,2,16]{1,4,3,2,0:T(8,128)(2,1)S(1)} %fusion.25) | data formatting | bytes 2097152 | tf_op jit(solution)/shard_map/convert_element_type | solution.py:31
  161.6 10.4 %reshape.143 = bf16[8,2,32768]{2,1,0:T(2,128)(2,1)S(1)} reshape(bf16[512,16,2,2,16]{4,3,2,1,0:T(2,128)(2,1)} %bitcast.48) | data formatting | bytes 2097152
  172.0 22.6 %all_to_all.36 = bf16[8,2,32768]{2,1,0:T(2,128)(2,1)S(1)} all-to-all(bf16[8,2,32768]{2,1,0:T(2,128)(2,1)S(1)} %reshape.143), channel_id=1, replica_groups=mesh['ang'=32,'rad'=8] {'rad'}, dimensions={0} | all-to-all | bytes 2097152 | tf_op jit(solution)/shard_map/all_to_all | solution.py:41
  194.7 7.5 %reshape.144 = bf16[512,16,2,2,16]{4,3,2,1,0:T(2,128)(2,1)} reshape(bf16[8,2,32768]{2,1,0:T(2,128)(2,1)S(1)} %all_to_all.36) | data formatting | bytes 2097152
  202.2 18.1 %copy.16 = bf16[16,8,64,2,2,16]{2,5,1,4,3,0:T(8,128)(2,1)S(1)} copy(bf16[16,8,64,2,2,16]{5,4,3,0,2,1:T(2,128)(2,1)} %bitcast.47) | data formatting | bytes 2097152 | tf_op jit(solution)/shard_map/all_to_all | solution.py:41
  220.3 1.7 copy.17
  222.0 0.0 copy-start.1
  222.0 3.3 %fusion.18 = f32[2,16,2,64,128]{4,1,2,0,3:T(8,128)S(1)} fusion(bf16[16,64,2,2,128]{4,0,3,2,1:T(8,128)(2,1)S(1)} %copy.17, bf16[64,128,128]{2,1,0:T(8,128)(2,1)} %param.7), kind=kOutput, calls=%fused_computation.24 | convolution fusion | flops 134217728 | bytes 5242880 | tf_op jit(solution)/shard_map/slkfr,lqr->ksflq/dot_general | solution.py:42
  225.3 2.5 %copy.18 = f32[2,16,2,64,128]{4,3,2,1,0:T(8,128)} copy(f32[2,16,2,64,128]{4,1,2,0,3:T(8,128)S(1)} %fusion.18) | data formatting | bytes 4194304 | tf_op jit(solution)/shard_map/slkfr,lqr->ksflq/transpose | solution.py:42
  227.8 0.0 copy-done.1
Async XLA Ops:
  0.0 14.6 %copy-start = (bf16[2,16,24,1536]{3,2,1,0:T(8,128)(2,1)S(1)}, bf16[2,16,24,1536]{3,2,1,0:T(8,128)(2,1)}, u32[]{:S(2)}) copy-start(bf16[2,16,24,1536]{3,2,1,0:T(8,128)(2,1)} %param.4) | copy-start | bytes 7077892
  44.0 48.9 %all-to-all-start = ((bf16[32,2,12288]{2,1,0:T(2,128)(2,1)}), bf16[32,2,12288]{2,1,0:T(2,128)(2,1)S(1)}, u32[]{:S(2)}, u32[]{:S(2)}) async-start(bf16[32,2,12288]{2,1,0:T(2,128)(2,1)} %reshape.141), calls=%async_computation | async-start | bytes 3145728 | tf_op jit(solution)/shard_map/all_to_all | solution.py:54
  222.0 5.8 %copy-start.1 = (bf16[2,16,24,1536]{3,2,1,0:T(8,128)(2,1)S(1)}, bf16[2,16,24,1536]{3,2,1,0:T(8,128)(2,1)}, u32[]{:S(2)}) copy-start(bf16[2,16,24,1536]{3,2,1,0:T(8,128)(2,1)} %param.4) | copy-start | bytes 7077892
where the time goes:
time: 229 us; the launch traced here: 228 us
  local copies, waits for them, and re-layouts  127 us (55%)
  waiting for transfers between devices  35.9 us (16%)
  blocking collectives  22.6 us (10%)
  matrix products  15.3 us (7%)
  other arithmetic  14.7 us (6%)
  starting transfers between devices  12 us (5%)
    unnamed x8, local copies, waits for them, and re-layouts  43.5 us
    all_to_all x1, waiting for transfers between devices, body(): lax.all_to_all(fourier, 'ang', split_axis=0, concat_axis=4, tiled=True)  35.9 us
    all_to_all x2, local copies, waits for them, and re-layouts, body(): lax.all_to_all(fourier, 'ang', split_axis=0, concat_axis=4, tiled=True)  32.2 us
    all_to_all x1, blocking collectives, solve_block(): lax.all_to_all(coefficients, 'rad', split_axis=1, concat_axis=4, tiled=True)  22.6 us
    all_to_all x2, local copies, waits for them, and re-layouts, solve_block(): lax.all_to_all(coefficients, 'rad', split_axis=1, concat_axis=4, tiled=True)  19.8 us
    convert_element_type x1, local copies, waits for them, and re-layouts, legendre_dense(): jnp.where(keeping, chosen, jnp.zeros_like(chosen)).astype(jnp.bfloat16)  14.8 us
    another operation x1, other arithmetic  14.6 us
    convert_element_type x1, local copies, waits for them, and re-layouts, body(): fourier = jnp.einsum('skj,frij->skfri', fourier_table, grid_field, prefer...  12.7 us
  transfers between devices with their start and end apart: 1, of which 1 were waited for; matrix products, arithmetic and copies ran while one was open for 0% of the time, Pallas kernels for 0%

commit v1 on v0

v1 whole, which is shorter than its diff:
```python
import functools
import math

import jax
import jax.numpy as jnp
import numpy as np
from jax import lax
from jax.experimental import pallas as pl
from jax.experimental.pallas import tpu as pltpu
from jax.sharding import PartitionSpec as P

LONS = 1536
HALF_LONS = LONS // 2
ORDERS = 512
PAIRS = ORDERS // 2
F32 = jnp.float32
BF16 = jnp.bfloat16


def transform_tables():
    longitude = np.arange(HALF_LONS, dtype=np.int64)[:, None]
    even = 2 * np.arange(PAIRS, dtype=np.int64)[None, :]
    tables = []
    for order in (even, ORDERS - 1 - even):
        angle = (longitude * order % LONS) * (2.0 * math.pi / LONS)
        columns = np.concatenate([np.cos(angle), -np.sin(angle)], axis=1)
        tables.append((columns / math.sqrt(LONS)).astype(np.float32).astype(BF16))
    return tables


def fourier_kernel(lats, order_ref, south_ref, x_ref, even_ref, odd_ref, out_ref, product, turned):
    rows = x_ref.shape[0]
    columns = rows // lats
    for start in range(0, rows, 256):
        near = x_ref[start : start + 256, :HALF_LONS].astype(F32)
        far = x_ref[start : start + 256, HALF_LONS:].astype(F32)
        for parity, table in enumerate((even_ref, odd_ref)):
            mixed = (near - far if parity else near + far).astype(BF16)
            result = jnp.dot(mixed, table[...], preferred_element_type=F32)
            for part in range(4):
                product[parity * 4 + part, start : start + 256, :] = result[:, part * 128 : part * 128 + 128]
    south = south_ref[0]

    def turn(row, _):
        placed = jnp.where(south == 1, lats - 1 - row, row)
        for half in range(2):
            picked = [product[2 * part + half, pl.ds(row, columns, stride=lats), :] for part in range(4)]
            block = jnp.concatenate(picked, axis=0).T
            turned[pl.ds(half * 128 * lats + placed, 128, stride=lats), :] = block
        return 0

    lax.fori_loop(0, lats, turn, 0)

    def place(step, _):
        picked = []
        for offset in range(2):
            order = order_ref[step * 4 + offset * 2]
            pair = jnp.where(order % 2 == 0, order, ORDERS - 1 - order) // 2
            picked.append(turned[pl.ds(pl.multiple_of(pair * lats, 8), lats), :])
        at = pl.ds(pl.multiple_of(step * 2 * lats, 16), 2 * lats)
        out_ref[at, :] = jnp.concatenate(picked, axis=0).astype(BF16)
        return 0

    lax.fori_loop(0, PAIRS // 2, place, 0)


def fourier_stage(slot_order, south, rows, lats):
    even, odd = transform_tables()
    smem = pl.BlockSpec(memory_space=pltpu.SMEM)
    vmem = pl.BlockSpec(memory_space=pltpu.VMEM)
    return pl.pallas_call(
        functools.partial(fourier_kernel, lats),
        out_shape=jax.ShapeDtypeStruct((PAIRS * lats, 128), BF16),
        in_specs=[smem, smem, vmem, vmem, vmem],
        out_specs=vmem,
        scratch_shapes=[
            pltpu.VMEM((8, rows.shape[0], 128), F32),
            pltpu.VMEM((PAIRS * lats, 128), F32),
        ],
        compiler_params=pltpu.CompilerParams(vmem_limit_bytes=48 * 2**20),
        name="fourier",
    )(slot_order, south, rows, jnp.asarray(even), jnp.asarray(odd))


def legendre_kernel(lats, order_ref, recv_ref, table_ref, out_ref):
    sources, _, _ = recv_ref.shape
    half = sources // 2
    step = pl.program_id(0)
    degrees = table_ref.shape[2]
    degree = lax.broadcasted_iota(jnp.int32, (64, degrees), 1)
    for pair in range(2):
        rows = slice(pair * lats, (pair + 1) * lats)
        pieces = [recv_ref[source, :, :].astype(F32)[rows] for source in range(sources)]
        north = jnp.concatenate(pieces[:half], axis=0)
        mirrored = jnp.concatenate(pieces[half:][::-1], axis=0)
        symmetric = (north + mirrored).T.astype(BF16)
        antisymmetric = (north - mirrored).T.astype(BF16)
        first = order_ref[(step * 2 + pair) * 2]
        first_odd = first % 2
        chosen = []
        for parity in range(2):
            order = jnp.where(first_odd == parity, first, ORDERS - 1 - first)
            slot = pair * 2 + jnp.where(first_odd == parity, 0, 1)
            wanted = slice(parity * 64, parity * 64 + 64)
            both = jnp.concatenate([symmetric[wanted], antisymmetric[wanted]], axis=0)
            result = jnp.dot(both, table_ref[slot], preferred_element_type=F32)
            kept = jnp.where(degree % 2 == parity, result[:64], result[64:])
            chosen.append(jnp.where(degree >= order, kept, 0.0))
        for block in range(degrees // 64):
            lanes = slice(block * 64, block * 64 + 64)
            joined = jnp.concatenate([chosen[0][:, lanes], chosen[1][:, lanes]], axis=1)
            out_ref[block, pair * 64 : pair * 64 + 64, :] = joined.astype(BF16)


def legendre_stage(orders, received, legendre, lats):
    sources, rows, _ = received.shape
    pairs = rows // lats
    slots, northern, degrees = legendre.shape
    return pl.pallas_call(
        functools.partial(legendre_kernel, lats),
        out_shape=jax.ShapeDtypeStruct((degrees // 64, pairs * 64, 128), BF16),
        grid=(pairs // 2,),
        in_specs=[
            pl.BlockSpec(memory_space=pltpu.SMEM),
            pl.BlockSpec((sources, 2 * lats, 128), lambda step: (0, step, 0)),
            pl.BlockSpec((4, northern, degrees), lambda step: (step, 0, 0)),
        ],
        out_specs=pl.BlockSpec((degrees // 64, 128, 128), lambda step: (0, step, 0)),
        compiler_params=pltpu.CompilerParams(vmem_limit_bytes=48 * 2**20),
        name="legendre",
    )(orders, received, legendre)


def solve_kernel(order_ref, recv_ref, inverse_ref, out_ref, turned):
    sources, rows, _ = recv_ref.shape
    pairs = rows // 64
    degrees = inverse_ref.shape[0]
    lines = out_ref.shape[0] // degrees
    for pair in range(pairs):
        first_odd = order_ref[pair * 2] % 2
        for part in range(4):
            rows = slice(pair * 64 + part * 16, pair * 64 + part * 16 + 16)
            block = jnp.concatenate([recv_ref[source, rows, :] for source in range(sources)], axis=0)
            block = block.astype(F32).T
            for parity in range(2):
                slot = pair * 2 + jnp.where(first_odd == parity, 0, 1)
                line = (part // 2) * (4 * pairs) + slot * 2 + part % 2
                at = pl.ds(pl.multiple_of(line * degrees, 64), degrees)
                turned[at, :] = block[parity * 64 : parity * 64 + 64]

    def solve(degree, _):
        picked = turned[pl.ds(degree, lines, stride=degrees), :].astype(BF16)
        result = lax.dot_general(
            picked, inverse_ref[degree], (((1,), (1,)), ((), ())), preferred_element_type=F32
        )
        out_ref[pl.ds(degree, lines, stride=degrees), :] = result
        return 0

    lax.fori_loop(0, degrees, solve, 0, unroll=8)


def solve_stage(orders, received, inverses):
    sources, rows, _ = received.shape
    degrees = inverses.shape[0]
    lines = rows // 64 * 8
    smem = pl.BlockSpec(memory_space=pltpu.SMEM)
    vmem = pl.BlockSpec(memory_space=pltpu.VMEM)
    return pl.pallas_call(
        solve_kernel,
        out_shape=jax.ShapeDtypeStruct((lines * degrees, 128), F32),
        in_specs=[smem, vmem, vmem],
        out_specs=vmem,
        scratch_shapes=[pltpu.VMEM((lines * degrees, 128), F32)],
        compiler_params=pltpu.CompilerParams(vmem_limit_bytes=48 * 2**20),
        name="solve",
    )(orders, received, inverses)


def body(grid_field, slot_order, legendre, inverses):
    fields, radii, lats, lons = grid_field.shape
    slots = legendre.shape[0]
    place = lax.axis_index("ang")
    count = lax.axis_size("ang")
    south = (place >= count // 2).astype(jnp.int32).reshape(1)
    orders = lax.dynamic_slice_in_dim(slot_order, place * slots, slots)
    fourier = fourier_stage(slot_order, south, grid_field.reshape(fields * radii * lats, lons), lats)
    sent = fourier.reshape(count, slots // 2 * lats, 128)
    received = lax.all_to_all(sent, "ang", split_axis=0, concat_axis=0)
    coefficients = legendre_stage(orders, received, legendre, lats)
    moved = lax.all_to_all(coefficients, "rad", split_axis=0, concat_axis=0)
    spectrum = solve_stage(orders, moved, inverses)
    return spectrum.reshape(2, slots, fields, inverses.shape[0], 128)


def solution(mesh):
    placed = (P(None, "rad", "ang", None), P(), P("ang", None, None), P("rad", None, None))
    return jax.shard_map(
        body,
        mesh=mesh,
        in_specs=placed,
        out_specs=P(None, "ang", None, "rad", None),
        check_vma=False,
    )
```

time: 229 us -> 95.6 us (0.42)
  local copies, waits for them, and re-layouts: 127 us -> 5.38 us
  Pallas kernels: 0 us -> 18.9 us
  matrix products: 15.3 us -> 0 us
  other arithmetic: 14.7 us -> 0 us
    all_to_all x4 -> x0, local copies, waits for them, and re-layouts: 52 us -> none  [the longest x2 32.2 us: body(): lax.all_to_all(fourier, 'ang', split_axis=0, concat_axis=4, tiled=True)]
    unnamed x8 -> x10, local copies, waits for them, and re-layouts: 43.5 us -> 4.62 us
    convert_element_type x2 -> x0, local copies, waits for them, and re-layouts: 27.5 us -> none  [the longest x1 14.8 us: legendre_dense(): jnp.where(keeping, chosen, jnp.zeros_like(chosen)).astype(jnp.bfloat16)]
    pallas_call x0 -> x3, Pallas kernels: none -> 18.9 us  [the longest x1 8.88 us: fourier_stage(): pl.pallas_call(functools.partial(fourier_kernel, lats), out_shape=jax.Sha...]
    dot_general x4 -> x0, matrix products: 15.3 us -> none  [the longest x1 4.02 us: legendre_dense(): jnp.einsum('shl,skfrh->slkfr', legendre, antisymmetric, preferred_element...]
    another operation x1 -> x0, other arithmetic: 14.6 us -> none
    transpose x1 -> x0, local copies, waits for them, and re-layouts: 2.55 us -> none  [solve_block(): jnp.einsum('slkfr,lqr->ksflq', moved, inverses, preferred_element_type=jn...]
  transfers between devices with their start and end apart: 1 -> 1, of which waited for: 1 -> 1; matrix products, arithmetic and copies ran while one was open for 0% -> 1% of each run, Pallas kernels for 0% -> 0%
where the time goes in v1:
time: 95.6 us; the launch traced here: 95.2 us
  waiting for transfers between devices  36 us (38%)
  blocking collectives  22.8 us (24%)
  Pallas kernels  18.9 us (20%)
  starting transfers between devices  12 us (13%)
  local copies, waits for them, and re-layouts  5.38 us (6%)
    all_to_all x1, waiting for transfers between devices, body(): received = lax.all_to_all(sent, 'ang', split_axis=0, concat_axis=0)  36 us
    all_to_all x1, blocking collectives, body(): moved = lax.all_to_all(coefficients, 'rad', split_axis=0, concat_axis=0)  22.8 us
    all_to_all x1, starting transfers between devices, body(): received = lax.all_to_all(sent, 'ang', split_axis=0, concat_axis=0)  12 us
    pallas_call x1, Pallas kernels, fourier_stage(): pl.pallas_call(functools.partial(fourier_kernel, lats), out_shape=jax.Sha...  8.88 us
    pallas_call x1, Pallas kernels, solve_stage(): pl.pallas_call(solve_kernel, out_shape=jax.ShapeDtypeStruct((lines * degr...  5.17 us
    pallas_call x1, Pallas kernels, legendre_stage(): pl.pallas_call(functools.partial(legendre_kernel, lats), out_shape=jax.Sh...  4.85 us
    unnamed x10, local copies, waits for them, and re-layouts  4.62 us
  transfers between devices with their start and end apart: 1, of which 1 were waited for; matrix products, arithmetic and copies ran while one was open for 1% of the time, Pallas kernels for 0%

profile of v1, /device:TPU:1, one launch (start us, length us, event | category | flops | bytes accessed | tf_op | source)
XLA Modules:
  0.0 95.2 jit_solution(17608901144394235765)
XLA Ops:
  0.0 0.0 copy-start
  0.0 1.7 %copy-done = bf16[2,16,24,1536]{3,2,1,0:T(8,128)(2,1)S(1)} copy-done((bf16[2,16,24,1536]{3,2,1,0:T(8,128)(2,1)S(1)}, bf16[2,16,24,1536]{3,2,1,0:T(8,128)(2,1)}, u32[]{:S(2)}) %copy-start) | copy-done | bytes 2359320
  1.7 0.0 copy-start.2
  1.7 1.1 %copy-done.2 = bf16[768,512]{1,0:T(8,128)(2,1)S(1)} copy-done((bf16[768,512]{1,0:T(8,128)(2,1)S(1)}, bf16[768,512]{1,0:T(8,128)(2,1)}, u32[]{:S(2)}) %copy-start.2) | copy-done | bytes 786456
  2.8 0.0 copy-start.3
  2.8 1.1 %copy-done.3 = bf16[768,512]{1,0:T(8,128)(2,1)S(1)} copy-done((bf16[768,512]{1,0:T(8,128)(2,1)S(1)}, bf16[768,512]{1,0:T(8,128)(2,1)}, u32[]{:S(2)}) %copy-start.3) | copy-done | bytes 786456
  3.9 0.0 copy-start.4
  3.9 0.7 copy-done.4
  4.6 8.9 %fourier.1 = bf16[6144,128]{1,0:T(8,128)(2,1)} custom-call(s32[512]{0:T(512)S(1)} %copy-done.4, s32[1]{0:T(128)} %bitcast.south_ref, bf16[768,1536]{1,0:T(8,128)(2,1)S(1)} %bitcast.4, bf16[768,512]{1,0:T(8,128)(2,1)S(1)} %copy-done.3, bf16[768,512]{1,0:T(8,128)(2,1)S(1)} %copy-done.2), custom_call_target="tpu_custom_call" | custom-call | tf_op jit(solution)/shard_map/fourier/pallas_call | solution.py:71
  13.5 12.0 %all-to-all-start = ((bf16[32,192,128]{2,1,0:T(8,128)(2,1)}), bf16[32,192,128]{2,1,0:T(8,128)(2,1)S(1)}, u32[]{:S(2)}, u32[]{:S(2)}) async-start(bf16[32,192,128]{2,1,0:T(8,128)(2,1)} %bitcast.2), calls=%async_computation | async-start | bytes 3145728 | tf_op jit(solution)/shard_map/all_to_all | solution.py:188
  25.5 0.8 dynamic_slice.3.order_ref
  26.3 36.0 %all-to-all-done.recv_ref = bf16[32,192,128]{2,1,0:T(8,128)(2,1)S(1)} async-done(((bf16[32,192,128]{2,1,0:T(8,128)(2,1)}), bf16[32,192,128]{2,1,0:T(8,128)(2,1)S(1)}, u32[]{:S(2)}, u32[]{:S(2)}) %all-to-all-start) | async-done | bytes 1572896 | tf_op jit(solution)/shard_map/all_to_all | solution.py:188
  62.3 4.8 %legendre.1 = bf16[8,512,128]{2,1,0:T(8,128)(2,1)S(1)} custom-call(s32[16]{0:T(128)S(1)} %dynamic_slice.3.order_ref, bf16[32,192,128]{2,1,0:T(8,128)(2,1)S(1)} %all-to-all-done.recv_ref, bf16[16,384,512]{2,1,0:T(8,128)(2,1)} %table_ref.1), custom_call_target="tpu_custom_call" | custom-call | tf_op jit(solution)/shard_map/legendre/pallas_call | solution.py:119
  67.2 0.0 copy-start.1
  67.2 22.8 %all_to_all.10.recv_ref = bf16[8,512,128]{2,1,0:T(8,128)(2,1)S(1)} all-to-all(bf16[8,512,128]{2,1,0:T(8,128)(2,1)S(1)} %legendre.1), channel_id=1, replica_groups=mesh['ang'=32,'rad'=8] {'rad'}, dimensions={0} | all-to-all | bytes 2097152 | tf_op jit(solution)/shard_map/all_to_all | solution.py:190
  90.0 0.0 copy-done.1
  90.0 5.2 %solve.1 = f32[4096,128]{1,0:T(8,128)} custom-call(s32[16]{0:T(128)S(1)} %dynamic_slice.3.order_ref, bf16[8,512,128]{2,1,0:T(8,128)(2,1)S(1)} %all_to_all.10.recv_ref, bf16[64,128,128]{2,1,0:T(8,128)(2,1)S(1)} %copy-done.1), custom_call_target="tpu_custom_call" | custom-call | tf_op jit(solution)/shard_map/solve/pallas_call | solution.py:168
Async XLA Ops:
  0.0 1.7 %copy-start = (bf16[2,16,24,1536]{3,2,1,0:T(8,128)(2,1)S(1)}, bf16[2,16,24,1536]{3,2,1,0:T(8,128)(2,1)}, u32[]{:S(2)}) copy-start(bf16[2,16,24,1536]{3,2,1,0:T(8,128)(2,1)} %param.6) | copy-start | bytes 7077892
  1.7 1.1 %copy-start.2 = (bf16[768,512]{1,0:T(8,128)(2,1)S(1)}, bf16[768,512]{1,0:T(8,128)(2,1)}, u32[]{:S(2)}) copy-start(bf16[768,512]{1,0:T(8,128)(2,1)} %constant.17.clone.odd_ref) | copy-start | bytes 2359300
  2.8 1.1 %copy-start.3 = (bf16[768,512]{1,0:T(8,128)(2,1)S(1)}, bf16[768,512]{1,0:T(8,128)(2,1)}, u32[]{:S(2)}) copy-start(bf16[768,512]{1,0:T(8,128)(2,1)} %constant.16.clone.even_ref) | copy-start | bytes 2359300
  3.9 0.7 copy-start.4
  13.5 48.8 %all-to-all-start = ((bf16[32,192,128]{2,1,0:T(8,128)(2,1)}), bf16[32,192,128]{2,1,0:T(8,128)(2,1)S(1)}, u32[]{:S(2)}, u32[]{:S(2)}) async-start(bf16[32,192,128]{2,1,0:T(8,128)(2,1)} %bitcast.2), calls=%async_computation | async-start | bytes 3145728 | tf_op jit(solution)/shard_map/all_to_all | solution.py:188
  67.2 22.8 %copy-start.1 = (bf16[64,128,128]{2,1,0:T(8,128)(2,1)S(1)}, bf16[64,128,128]{2,1,0:T(8,128)(2,1)}, u32[]{:S(2)}) copy-start(bf16[64,128,128]{2,1,0:T(8,128)(2,1)} %inverse_ref.1) | copy-start | bytes 6291460

commit v2 on v0

v2 whole, which is shorter than its diff:
```python
import functools
import math

import jax
import jax.numpy as jnp
import numpy as np
from jax import lax
from jax.experimental import pallas as pl
from jax.experimental.pallas import tpu as pltpu
from jax.sharding import PartitionSpec as P

LONS = 1536
HALF_LONS = LONS // 2
ORDERS = 512
PAIRS = ORDERS // 2
NA, NR = 32, 8
F32 = jnp.float32
BF16 = jnp.bfloat16
SMEM = pl.BlockSpec(memory_space=pltpu.SMEM)
VMEM = pl.BlockSpec(memory_space=pltpu.VMEM)
HBM = pl.BlockSpec(memory_space=pltpu.HBM)
PARAMS = pltpu.CompilerParams(vmem_limit_bytes=24 * 2**20)
ROWS = 256


def transform_tables():
    longitude = np.arange(HALF_LONS, dtype=np.int64)[:, None]
    even = 2 * np.arange(PAIRS, dtype=np.int64)[None, :]
    tables = []
    for order in (even, ORDERS - 1 - even):
        angle = (longitude * order % LONS) * (2.0 * math.pi / LONS)
        columns = np.concatenate([np.cos(angle), -np.sin(angle)], axis=1)
        tables.append((columns / math.sqrt(LONS)).astype(np.float32).astype(BF16))
    return np.stack(tables)


def fourier_kernel(lats, order_ref, x_hbm, table_hbm, out_ref, x_ref, table_ref, product, turned, sems):
    place = lax.axis_index("ang")
    rows = x_ref.shape[0]
    columns = rows // lats
    copies = []
    for parity in range(2):
        copies.append(pltpu.make_async_copy(table_hbm.at[parity], table_ref.at[parity], sems.at[parity]))
    for index, start in enumerate(range(0, rows, ROWS)):
        at = pl.ds(start, ROWS)
        copies.append(pltpu.make_async_copy(x_hbm.at[at], x_ref.at[at], sems.at[2 + index]))
    for copy in (copies[0], copies[2], copies[1], *copies[3:]):
        copy.start()
    for index, start in enumerate(range(0, rows, ROWS)):
        copies[2 + index].wait()
        near = x_ref[start : start + ROWS, :HALF_LONS].astype(F32)
        far = x_ref[start : start + ROWS, HALF_LONS:].astype(F32)
        for parity in range(2):
            if start == 0:
                copies[parity].wait()
            mixed = (near - far if parity else near + far).astype(BF16)
            result = jnp.dot(mixed, table_ref[parity], preferred_element_type=F32)
            for part in range(4):
                product[parity * 4 + part, start : start + ROWS, :] = result[:, part * 128 : part * 128 + 128]

    def turn(row, _):
        placed = jnp.where(place >= NA // 2, lats - 1 - row, row)
        for half in range(2):
            picked = [product[2 * part + half, pl.ds(row, columns, stride=lats), :] for part in range(4)]
            block = jnp.concatenate(picked, axis=0).T
            turned[pl.ds(half * 128 * lats + placed, 128, stride=lats), :] = block
        return 0

    lax.fori_loop(0, lats, turn, 0, unroll=8)
    pairs = PAIRS // NA

    def put(device, _):
        for local in range(0, pairs, 2):
            picked = []
            for offset in range(2):
                order = order_ref[(device * pairs + local + offset) * 2]
                pair = lax.shift_right_logical(order ^ ((order & 1) * (ORDERS - 1)), 1)
                picked.append(turned[pl.ds(pl.multiple_of(pair * lats, 8), lats), :])
            out_ref[device, local * lats : (local + 2) * lats, :] = jnp.concatenate(picked, axis=0).astype(BF16)
        return 0

    lax.fori_loop(0, NA, put, 0, unroll=2)


def fourier_stage(slot_order, rows, lats):
    table = transform_tables()
    return pl.pallas_call(
        functools.partial(fourier_kernel, lats),
        out_shape=jax.ShapeDtypeStruct((NA, PAIRS // NA * lats, 128), BF16),
        in_specs=[SMEM, HBM, HBM],
        out_specs=VMEM,
        scratch_shapes=[
            pltpu.VMEM(rows.shape, BF16),
            pltpu.VMEM(table.shape, BF16),
            pltpu.VMEM((8, rows.shape[0], 128), F32),
            pltpu.VMEM((PAIRS * lats, 128), F32),
            pltpu.SemaphoreType.DMA((2 + rows.shape[0] // ROWS,)),
        ],
        compiler_params=pltpu.CompilerParams(vmem_limit_bytes=60 * 2**20),
        name="fourier",
    )(slot_order, rows, jnp.asarray(table))


def legendre_kernel(lats, order_ref, table_ref, received, out_ref):
    place = lax.axis_index("ang")
    slots, _, degrees = table_ref.shape
    half = NA // 2
    degree = lax.broadcasted_iota(jnp.int32, (64, degrees), 1)

    def couple(step, _):
        at = pl.ds(pl.multiple_of(step * 2 * lats, 16), 2 * lats)
        pieces = [received[source, at, :].astype(F32) for source in range(2 * half)]
        for pair in range(2):
            rows = slice(pair * lats, (pair + 1) * lats)
            north = jnp.concatenate([piece[rows] for piece in pieces[:half]], axis=0)
            mirrored = jnp.concatenate([piece[rows] for piece in pieces[half:][::-1]], axis=0)
            symmetric = (north + mirrored).astype(BF16).T
            antisymmetric = (north - mirrored).astype(BF16).T
            first = step * 4 + pair * 2
            order_here = order_ref[place * slots + first]
            first_odd = order_here % 2
            chosen = []
            for parity in range(2):
                order = jnp.where(first_odd == parity, order_here, ORDERS - 1 - order_here)
                slot = first + jnp.where(first_odd == parity, 0, 1)
                wanted = slice(parity * 64, parity * 64 + 64)
                both = jnp.concatenate([symmetric[wanted], antisymmetric[wanted]], axis=0)
                result = jnp.dot(both, table_ref[slot], preferred_element_type=F32)
                kept = jnp.where(degree % 2 == parity, result[:64], result[64:])
                chosen.append(jnp.where(degree >= order, kept, 0.0).astype(BF16))
            out_at = pl.ds(pl.multiple_of(step * 128 + pair * 64, 64), 64)
            for block in range(NR):
                lanes = slice(block * 64, block * 64 + 64)
                joined = jnp.concatenate([chosen[0][:, lanes], chosen[1][:, lanes]], axis=1)
                out_ref[block, out_at, :] = joined
        return 0

    lax.fori_loop(0, slots // 4, couple, 0, unroll=4)


def legendre_stage(slot_order, received, legendre, lats):
    slots, _, degrees = legendre.shape
    return pl.pallas_call(
        functools.partial(legendre_kernel, lats),
        out_shape=jax.ShapeDtypeStruct((NR, slots * 32, 128), BF16),
        in_specs=[SMEM, VMEM, VMEM],
        out_specs=VMEM,
        compiler_params=PARAMS,
        name="legendre",
    )(slot_order, legendre, received)


def solve_kernel(order_ref, inverse_ref, received, out_hbm, turned, solved, sems):
    place = lax.axis_index("ang")
    degrees = inverse_ref.shape[0]
    lines = solved.shape[1]
    pairs = lines // 8
    for pair in range(pairs):
        first_odd = order_ref[(place * pairs + pair) * 2] & 1
        for part in range(4):
            at = slice(pair * 64 + part * 16, pair * 64 + part * 16 + 16)
            block = jnp.concatenate([received[source, at, :] for source in range(NR)], axis=0)
            block = block.astype(F32).T
            for parity in range(2):
                slot = pair * 2 + (first_odd ^ parity)
                line = (part // 2) * (4 * pairs) + slot * 2 + part % 2
                turned[pl.ds(pl.multiple_of(line * 64, 64), 64), :] = block[parity * 64 : parity * 64 + 64]

    def copy(group):
        at = pl.ds(pl.multiple_of(group * 8, 8), 8)
        return pltpu.make_async_copy(solved.at[group], out_hbm.at[:, at], sems.at[group])

    def solve(group, _):
        for degree in range(8):
            picked = turned[pl.ds(group * 8 + degree, lines, stride=64), :].astype(BF16)
            solved[group, :, degree, :] = lax.dot_general(
                picked, inverse_ref[group * 8 + degree], (((1,), (1,)), ((), ())), preferred_element_type=F32
            )
        copy(group).start()
        return 0

    lax.fori_loop(0, degrees // 8, solve, 0)
    for group in range(degrees // 8):
        copy(group).wait()


def solve_stage(slot_order, received, inverses):
    degrees = inverses.shape[0]
    lines = received.shape[1] // 8
    return pl.pallas_call(
        solve_kernel,
        out_shape=jax.ShapeDtypeStruct((lines, degrees, 128), F32),
        in_specs=[SMEM, VMEM, VMEM],
        out_specs=HBM,
        scratch_shapes=[
            pltpu.VMEM((lines * degrees, 128), F32),
            pltpu.VMEM((degrees // 8, lines, 8, 128), F32),
            pltpu.SemaphoreType.DMA((degrees // 8,)),
        ],
        compiler_params=PARAMS,
        name="solve",
    )(slot_order, inverses, received)


def body(grid_field, slot_order, legendre, inverses):
    fields, radii, lats, lons = grid_field.shape
    slots = legendre.shape[0]
    sent = fourier_stage(slot_order, grid_field.reshape(fields * radii * lats, lons), lats)
    received = lax.all_to_all(sent, "ang", split_axis=0, concat_axis=0)
    coefficients = legendre_stage(slot_order, received, legendre, lats)
    moved = lax.all_to_all(coefficients, "rad", split_axis=0, concat_axis=0)
    spectrum = solve_stage(slot_order, moved, inverses)
    return spectrum.reshape(2, slots, fields, inverses.shape[0], 128)


def solution(mesh):
    placed = (P(None, "rad", "ang", None), P(), P("ang", None, None), P("rad", None, None))
    return jax.shard_map(
        body,
        mesh=mesh,
        in_specs=placed,
        out_specs=P(None, "ang", None, "rad", None),
        check_vma=False,
    )
```

time: 229 us -> 88.1 us (0.38)
  local copies, waits for them, and re-layouts: 127 us -> 2.8 us
  blocking collectives: 22.6 us -> 71.6 us
  waiting for transfers between devices: 35.9 us -> 0 us
  matrix products: 15.3 us -> 0 us
  other arithmetic: 14.7 us -> 0 us
  Pallas kernels: 0 us -> 13.2 us
  starting transfers between devices: 12 us -> 0 us
    all_to_all x4 -> x0, local copies, waits for them, and re-layouts: 52 us -> none  [the longest x2 32.2 us: body(): lax.all_to_all(fourier, 'ang', split_axis=0, concat_axis=4, tiled=True)]
    all_to_all x1 -> x2, blocking collectives: 22.6 us -> 71.6 us  [the longest x1 48.7 us: body(): received = lax.all_to_all(sent, 'ang', split_axis=0, concat_axis=0)]
    unnamed x8 -> x6, local copies, waits for them, and re-layouts: 43.5 us -> 2.8 us
    all_to_all x1 -> x0, waiting for transfers between devices: 35.9 us -> none  [body(): lax.all_to_all(fourier, 'ang', split_axis=0, concat_axis=4, tiled=True)]
    convert_element_type x2 -> x0, local copies, waits for them, and re-layouts: 27.5 us -> none  [the longest x1 14.8 us: legendre_dense(): jnp.where(keeping, chosen, jnp.zeros_like(chosen)).astype(jnp.bfloat16)]
    dot_general x4 -> x0, matrix products: 15.3 us -> none  [the longest x1 4.02 us: legendre_dense(): jnp.einsum('shl,skfrh->slkfr', legendre, antisymmetric, preferred_element...]
    another operation x1 -> x0, other arithmetic: 14.6 us -> none
    pallas_call x0 -> x3, Pallas kernels: none -> 13.2 us  [the longest x1 6.92 us: fourier_stage(): pl.pallas_call(functools.partial(fourier_kernel, lats), out_shape=jax.Sha...]
  transfers between devices with their start and end apart: 1 -> 0, of which waited for: 1 -> 0; matrix products, arithmetic and copies ran while one was open for 0% -> 0% of each run, Pallas kernels for 0% -> 0%
where the time goes in v2:
time: 88.1 us; the launch traced here: 87.6 us
  blocking collectives  71.6 us (81%)
  Pallas kernels  13.2 us (15%)
  local copies, waits for them, and re-layouts  2.8 us (3%)
    all_to_all x1, blocking collectives, body(): received = lax.all_to_all(sent, 'ang', split_axis=0, concat_axis=0)  48.7 us
    all_to_all x1, blocking collectives, body(): moved = lax.all_to_all(coefficients, 'rad', split_axis=0, concat_axis=0)  22.9 us
    pallas_call x1, Pallas kernels, fourier_stage(): pl.pallas_call(functools.partial(fourier_kernel, lats), out_shape=jax.Sha...  6.92 us
    pallas_call x1, Pallas kernels, solve_stage(): pl.pallas_call(solve_kernel, out_shape=jax.ShapeDtypeStruct((lines, degre...  4.16 us
    unnamed x6, local copies, waits for them, and re-layouts  2.8 us
    pallas_call x1, Pallas kernels, legendre_stage(): pl.pallas_call(functools.partial(legendre_kernel, lats), out_shape=jax.Sh...  2.08 us

profile of v2, /device:TPU:1, one launch (start us, length us, event | category | flops | bytes accessed | tf_op | source)
XLA Modules:
  0.0 87.6 jit_solution(16043454091292425089)
XLA Ops:
  0.0 6.9 %fourier.1 = bf16[32,192,128]{2,1,0:T(8,128)(2,1)} custom-call(s32[512]{0:T(512)} %order_ref.5, bf16[768,1536]{1,0:T(8,128)(2,1)} %bitcast.2, bf16[2,768,512]{2,1,0:T(8,128)(2,1)} %constant.2.clone.table_hbm), custom_call_target="tpu_custom_call" | custom-call | tf_op jit(solution)/shard_map/fourier/pallas_call | solution.py:87
  6.9 0.0 copy-start.2
  6.9 48.7 %all_to_all.10.received = bf16[32,192,128]{2,1,0:T(8,128)(2,1)S(1)} all-to-all(bf16[32,192,128]{2,1,0:T(8,128)(2,1)} %fourier.1), channel_id=1, replica_groups=mesh['ang'=32,'rad'=8] {'ang'}, dimensions={0} | all-to-all | bytes 3145728 | tf_op jit(solution)/shard_map/all_to_all | solution.py:209
  55.7 0.0 copy-done.2
  55.7 0.0 copy-start
  55.7 2.8 %copy-done = bf16[16,384,512]{2,1,0:T(8,128)(2,1)S(1)} copy-done((bf16[16,384,512]{2,1,0:T(8,128)(2,1)S(1)}, bf16[16,384,512]{2,1,0:T(8,128)(2,1)}, u32[]{:S(2)}) %copy-start) | copy-done | bytes 6291480
  58.5 2.1 %legendre.1 = bf16[8,512,128]{2,1,0:T(8,128)(2,1)S(1)} custom-call(s32[512]{0:T(512)S(1)} %copy-done.2, bf16[16,384,512]{2,1,0:T(8,128)(2,1)S(1)} %copy-done, bf16[32,192,128]{2,1,0:T(8,128)(2,1)S(1)} %all_to_all.10.received), custom_call_target="tpu_custom_call" | custom-call | tf_op jit(solution)/shard_map/legendre/pallas_call | solution.py:143
  60.6 0.0 copy-start.1
  60.6 22.9 %all_to_all.11.received = bf16[8,512,128]{2,1,0:T(8,128)(2,1)S(1)} all-to-all(bf16[8,512,128]{2,1,0:T(8,128)(2,1)S(1)} %legendre.1), channel_id=1, replica_groups=mesh['ang'=32,'rad'=8] {'rad'}, dimensions={0} | all-to-all | bytes 2097152 | tf_op jit(solution)/shard_map/all_to_all | solution.py:211
  83.5 0.0 copy-done.1
  83.5 4.2 %solve.1 = f32[64,64,128]{2,1,0:T(8,128)} custom-call(s32[512]{0:T(512)S(1)} %copy-done.2, bf16[64,128,128]{2,1,0:T(8,128)(2,1)S(1)} %copy-done.1, bf16[8,512,128]{2,1,0:T(8,128)(2,1)S(1)} %all_to_all.11.received), custom_call_target="tpu_custom_call" | custom-call | tf_op jit(solution)/shard_map/solve/pallas_call | solution.py:190
Async XLA Ops:
  6.9 48.8 %copy-start.2 = (s32[512]{0:T(512)S(1)}, s32[512]{0:T(512)}, u32[]{:S(2)}) copy-start(s32[512]{0:T(512)} %order_ref.5) | copy-start | bytes 6148
  55.7 2.8 %copy-start = (bf16[16,384,512]{2,1,0:T(8,128)(2,1)S(1)}, bf16[16,384,512]{2,1,0:T(8,128)(2,1)}, u32[]{:S(2)}) copy-start(bf16[16,384,512]{2,1,0:T(8,128)(2,1)} %table_ref.1) | copy-start | bytes 18874372
  60.6 22.9 %copy-start.1 = (bf16[64,128,128]{2,1,0:T(8,128)(2,1)S(1)}, bf16[64,128,128]{2,1,0:T(8,128)(2,1)}, u32[]{:S(2)}) copy-start(bf16[64,128,128]{2,1,0:T(8,128)(2,1)} %inverse_ref.1) | copy-start | bytes 6291460

commit v3 on v2

--- a/solution.py
+++ b/solution.py
@@ -14,6 +14,8 @@
 ORDERS = 512
 PAIRS = ORDERS // 2
 NA, NR = 32, 8
+NX, NC = 4, 2
+PARTS = (8,)
 F32 = jnp.float32
 BF16 = jnp.bfloat16
 SMEM = pl.BlockSpec(memory_space=pltpu.SMEM)
@@ -96,79 +98,115 @@
             pltpu.VMEM((PAIRS * lats, 128), F32),
             pltpu.SemaphoreType.DMA((2 + rows.shape[0] // ROWS,)),
         ],
-        compiler_params=pltpu.CompilerParams(vmem_limit_bytes=60 * 2**20),
+        compiler_params=pltpu.CompilerParams(vmem_limit_bytes=52 * 2**20),
         name="fourier",
     )(slot_order, rows, jnp.asarray(table))
 
 
-def legendre_kernel(lats, order_ref, table_ref, received, out_ref):
+def legendre_kernel(lats, order_ref, table_ref, received, *refs):
+    outs, (sent, symmetric, antisymmetric) = refs[:-3], refs[-3:]
     place = lax.axis_index("ang")
+    column = lax.axis_index("rad")
+    here_x, here_c = column // NC, column % NC
     slots, _, degrees = table_ref.shape
     half = NA // 2
     degree = lax.broadcasted_iota(jnp.int32, (64, degrees), 1)
 
-    def couple(step, _):
-        at = pl.ds(pl.multiple_of(step * 2 * lats, 16), 2 * lats)
+    def upper_first(pair):
+        return lax.shift_right_logical(order_ref[place * slots + pair * 2], 8)
+
+    for step in range(slots // 4):
+        at = slice(step * 2 * lats, (step + 1) * 2 * lats)
         pieces = [received[source, at, :].astype(F32) for source in range(2 * half)]
-        for pair in range(2):
-            rows = slice(pair * lats, (pair + 1) * lats)
+        for pair in range(step * 2, step * 2 + 2):
+            rows = slice(pair % 2 * lats, (pair % 2 + 1) * lats)
             north = jnp.concatenate([piece[rows] for piece in pieces[:half]], axis=0)
             mirrored = jnp.concatenate([piece[rows] for piece in pieces[half:][::-1]], axis=0)
-            symmetric = (north + mirrored).astype(BF16).T
-            antisymmetric = (north - mirrored).astype(BF16).T
-            first = step * 4 + pair * 2
-            order_here = order_ref[place * slots + first]
-            first_odd = order_here % 2
-            chosen = []
-            for parity in range(2):
-                order = jnp.where(first_odd == parity, order_here, ORDERS - 1 - order_here)
-                slot = first + jnp.where(first_odd == parity, 0, 1)
-                wanted = slice(parity * 64, parity * 64 + 64)
-                both = jnp.concatenate([symmetric[wanted], antisymmetric[wanted]], axis=0)
-                result = jnp.dot(both, table_ref[slot], preferred_element_type=F32)
-                kept = jnp.where(degree % 2 == parity, result[:64], result[64:])
-                chosen.append(jnp.where(degree >= order, kept, 0.0).astype(BF16))
-            out_at = pl.ds(pl.multiple_of(step * 128 + pair * 64, 64), 64)
-            for block in range(NR):
-                lanes = slice(block * 64, block * 64 + 64)
-                joined = jnp.concatenate([chosen[0][:, lanes], chosen[1][:, lanes]], axis=1)
-                out_ref[block, out_at, :] = joined
-        return 0
-
-    lax.fori_loop(0, slots // 4, couple, 0, unroll=4)
+            symmetric[pair] = (north + mirrored).astype(BF16).T
+            antisymmetric[pair] = (north - mirrored).astype(BF16).T
+
+    for pair in range(slots // 2):
+        first = order_ref[place * slots + pair * 2]
+        lower = jnp.where(first >= ORDERS // 2, ORDERS - 1 - first, first)
+        chosen = []
+        for which, order in enumerate((lower, ORDERS - 1 - lower)):
+            begin = which * (degrees // 2)
+            wanted = pl.ds(pl.multiple_of((order & 1) * 64, 64), 64)
+            both = jnp.concatenate([symmetric[pair, wanted], antisymmetric[pair, wanted]], axis=0)
+            result = jnp.dot(both, table_ref[pair * 2 + (upper_first(pair) ^ which), :, begin:], preferred_element_type=F32)
+            here = degree[:, begin:]
+            kept = jnp.where(((here ^ order) & 1) == 0, result[:64], result[64:])
+            chosen.append(jnp.where(here >= order, kept, 0.0).astype(BF16))
+        out_at = slice(pair * 64, pair * 64 + 64)
+        for block in range(NR):
+            left = chosen[0][:, block * 64 : block * 64 + 64]
+            right = jnp.zeros_like(left)
+            if block * 64 >= degrees // 2:
+                right = chosen[1][:, block * 64 - degrees // 2 : block * 64 - degrees // 2 + 64]
+            step_x = (block // NC - here_x) & (NX - 1)
+            sent[step_x * NC + ((block % NC) ^ here_c), out_at, :] = jnp.concatenate([left, right], axis=1)
+    start = 0
+    for part in range(len(PARTS)):
+        rows = slice(start, start + PARTS[part] * 64)
+        for step_x in range(NX):
+            for step_c in range(NC):
+                outs[part * NX + step_x][step_c] = sent[step_x * NC + step_c, rows, :]
+        start += PARTS[part] * 64
 
 
 def legendre_stage(slot_order, received, legendre, lats):
-    slots, _, degrees = legendre.shape
-    return pl.pallas_call(
+    slots, _, _ = legendre.shape
+    shapes = [jax.ShapeDtypeStruct((NC, pairs * 64, 128), BF16) for pairs in PARTS for _ in range(NX)]
+    sent = pl.pallas_call(
         functools.partial(legendre_kernel, lats),
-        out_shape=jax.ShapeDtypeStruct((NR, slots * 32, 128), BF16),
+        out_shape=shapes,
         in_specs=[SMEM, VMEM, VMEM],
-        out_specs=VMEM,
-        compiler_params=PARAMS,
+        out_specs=[VMEM] * len(shapes),
+        scratch_shapes=[
+            pltpu.VMEM((NR, slots * 32, 128), BF16),
+            pltpu.VMEM((slots // 2, 128, legendre.shape[1]), BF16),
+            pltpu.VMEM((slots // 2, 128, legendre.shape[1]), BF16),
+        ],
+        compiler_params=pltpu.CompilerParams(vmem_limit_bytes=24 * 2**20),
         name="legendre",
     )(slot_order, legendre, received)
-
-
-def solve_kernel(order_ref, inverse_ref, received, out_hbm, turned, solved, sems):
+    return [sent[part * NX : (part + 1) * NX] for part in range(len(PARTS))]
+
+
+def solve_kernel(first_pair, order_ref, inverse_ref, *refs):
+    mine, others, (out_hbm, received, turned, solved, sems) = refs[:NX], refs[NX : 2 * NX], refs[-5:]
     place = lax.axis_index("ang")
+    column = lax.axis_index("rad")
+    here_x, here_c = column // NC, column % NC
     degrees = inverse_ref.shape[0]
     lines = solved.shape[1]
     pairs = lines // 8
+    for step_x in range(NX):
+        source = ((here_x - step_x) & (NX - 1)) * NC + here_c
+        received[source] = mine[step_x][0]
+        received[source ^ 1] = others[step_x][...]
     for pair in range(pairs):
-        first_odd = order_ref[(place * pairs + pair) * 2] & 1
+        upper_first = lax.shift_right_logical(order_ref[(place * sum(PARTS) + first_pair + pair) * 2], 8)
         for part in range(4):
             at = slice(pair * 64 + part * 16, pair * 64 + part * 16 + 16)
             block = jnp.concatenate([received[source, at, :] for source in range(NR)], axis=0)
             block = block.astype(F32).T
-            for parity in range(2):
-                slot = pair * 2 + (first_odd ^ parity)
+            for which in range(2):
+                slot = pair * 2 + (upper_first ^ which)
                 line = (part // 2) * (4 * pairs) + slot * 2 + part % 2
-                turned[pl.ds(pl.multiple_of(line * 64, 64), 64), :] = block[parity * 64 : parity * 64 + 64]
-
-    def copy(group):
+                turned[pl.ds(pl.multiple_of(line * 64, 64), 64), :] = block[which * 64 : which * 64 + 64]
+
+    def copies(group):
         at = pl.ds(pl.multiple_of(group * 8, 8), 8)
-        return pltpu.make_async_copy(solved.at[group], out_hbm.at[:, at], sems.at[group])
+        whole = out_hbm.shape[0] // 2
+        return [
+            pltpu.make_async_copy(
+                solved.at[group, pl.ds(k * (lines // 2), lines // 2)],
+                out_hbm.at[pl.ds(k * whole + first_pair * 4, lines // 2), at],
+                sems.at[group, k],
+            )
+            for k in range(2)
+        ]
 
     def solve(group, _):
         for degree in range(8):
@@ -176,30 +214,56 @@
             solved[group, :, degree, :] = lax.dot_general(
                 picked, inverse_ref[group * 8 + degree], (((1,), (1,)), ((), ())), preferred_element_type=F32
             )
-        copy(group).start()
+        for copy in copies(group):
+            copy.start()
         return 0
 
-    lax.fori_loop(0, degrees // 8, solve, 0)
+    lax.fori_loop(0, degrees // 8, solve, 0, unroll=2)
     for group in range(degrees // 8):
-        copy(group).wait()
-
-
-def solve_stage(slot_order, received, inverses):
+        for copy in copies(group):
+            copy.wait()
+
+
+def solve_stage(slot_order, mine, others, inverses, first_pair, earlier):
     degrees = inverses.shape[0]
-    lines = received.shape[1] // 8
+    lines = mine[0].shape[1] // 8
+    operands = [slot_order, inverses, *mine, *others]
+    specs = [SMEM] + [VMEM] * (len(operands) - 1)
+    aliases = {}
+    if earlier is not None:
+        aliases = {len(operands): 0}
+        operands.append(earlier)
+        specs.append(HBM)
     return pl.pallas_call(
-        solve_kernel,
-        out_shape=jax.ShapeDtypeStruct((lines, degrees, 128), F32),
-        in_specs=[SMEM, VMEM, VMEM],
+        functools.partial(solve_kernel, first_pair),
+        out_shape=jax.ShapeDtypeStruct((sum(PARTS) * 8, degrees, 128), F32),
+        in_specs=specs,
         out_specs=HBM,
+        input_output_aliases=aliases,
         scratch_shapes=[
+            pltpu.VMEM((NR, lines * 8, 128), BF16),
             pltpu.VMEM((lines * degrees, 128), F32),
             pltpu.VMEM((degrees // 8, lines, 8, 128), F32),
-            pltpu.SemaphoreType.DMA((degrees // 8,)),
+            pltpu.SemaphoreType.DMA((degrees // 8, 2)),
         ],
         compiler_params=PARAMS,
         name="solve",
-    )(slot_order, inverses, received)
+    )(*operands)
+
+
+def along_x(parts):
+    moved = [None] * NX
+    moved[0] = parts[0]
+    for step in (2, 1, 3):
+        moved[step] = lax.ppermute(
+            parts[step], "rad", [(a, (a + step * NC) % (NX * NC)) for a in range(NX * NC)]
+        )
+    return moved
+
+
+def along_core(parts):
+    swap = [(a, a ^ 1) for a in range(NX * NC)]
+    return [lax.ppermute(part[1], "rad", swap) for part in parts]
 
 
 def body(grid_field, slot_order, legendre, inverses):
@@ -207,9 +271,11 @@
     slots = legendre.shape[0]
     sent = fourier_stage(slot_order, grid_field.reshape(fields * radii * lats, lons), lats)
     received = lax.all_to_all(sent, "ang", split_axis=0, concat_axis=0)
-    coefficients = legendre_stage(slot_order, received, legendre, lats)
-    moved = lax.all_to_all(coefficients, "rad", split_axis=0, concat_axis=0)
-    spectrum = solve_stage(slot_order, moved, inverses)
+    parts = [along_x(part) for part in legendre_stage(slot_order, received, legendre, lats)]
+    spectrum, first = None, 0
+    for part, pairs in zip(parts, PARTS):
+        spectrum = solve_stage(slot_order, part, along_core(part), inverses, first, spectrum)
+        first += pairs
     return spectrum.reshape(2, slots, fields, inverses.shape[0], 128)
 
 

time: 88.1 us -> 80.8 us (0.917)
  blocking collectives: 71.6 us -> 48.5 us
  starting transfers between devices: 0 us -> 17.8 us
  local copies, waits for them, and re-layouts: 2.8 us -> 0.73 us
  waiting for transfers between devices: 0 us -> 0.99 us
  Pallas kernels: 13.2 us -> 12.3 us
    all_to_all x1 -> x0, blocking collectives: 22.9 us -> none  [body(): moved = lax.all_to_all(coefficients, 'rad', split_axis=0, concat_axis=0)]
    ppermute x0 -> x7, starting transfers between devices: none -> 17.8 us  [the longest x4 12.9 us: along_core(): return [lax.ppermute(part[1], 'rad', swap) for part in parts]]
    unnamed x6, local copies, waits for them, and re-layouts: 2.8 us -> 0.69 us
    pallas_call x1, Pallas kernels: 6.92 us -> 5.89 us  [fourier_stage(): pl.pallas_call(functools.partial(fourier_kernel, lats), out_shape=jax.Sha...]
    ppermute x0 -> x7, waiting for transfers between devices: none -> 0.99 us  [the longest x4 0.98 us: along_core(): return [lax.ppermute(part[1], 'rad', swap) for part in parts]]
  transfers between devices with their start and end apart: 0 -> 7, of which waited for: 0 -> 1; matrix products, arithmetic and copies ran while one was open for 0% -> 0% of each run, Pallas kernels for 0% -> 0%
where the time goes in v3:
time: 80.8 us; the launch traced here: 80.4 us
  blocking collectives  48.5 us (60%)
  starting transfers between devices  17.8 us (22%)
  Pallas kernels  12.3 us (15%)
  waiting for transfers between devices  0.99 us (1%)
    all_to_all x1, blocking collectives, body(): received = lax.all_to_all(sent, 'ang', split_axis=0, concat_axis=0)  48.5 us
    ppermute x4, starting transfers between devices, along_core(): return [lax.ppermute(part[1], 'rad', swap) for part in parts]  12.9 us
    pallas_call x1, Pallas kernels, fourier_stage(): pl.pallas_call(functools.partial(fourier_kernel, lats), out_shape=jax.Sha...  5.89 us
    ppermute x3, starting transfers between devices, along_x(): lax.ppermute(parts[step], 'rad', [(a, (a + step * NC) % (NX * NC)) for a...  4.91 us
    pallas_call x1, Pallas kernels, solve_stage(): pl.pallas_call(functools.partial(solve_kernel, first_pair), out_shape=jax...  4.26 us
    pallas_call x1, Pallas kernels, legendre_stage(): pl.pallas_call(functools.partial(legendre_kernel, lats), out_shape=shapes...  2.11 us
  transfers between devices with their start and end apart: 7, of which 1 were waited for; matrix products, arithmetic and copies ran while one was open for 0% of the time, Pallas kernels for 0%

profile of v3, /device:TPU:1, one launch (start us, length us, event | category | flops | bytes accessed | tf_op | source)
XLA Modules:
  0.0 80.4 jit_solution(11420168118784942936)
XLA Ops:
  0.0 0.0 copy-start.2
  0.0 0.7 copy-done.2
  0.7 0.0 copy-start
  0.7 5.9 %fourier.1 = bf16[32,192,128]{2,1,0:T(8,128)(2,1)S(1)} custom-call(s32[512]{0:T(512)S(1)} %copy-done.2, bf16[768,1536]{1,0:T(8,128)(2,1)} %bitcast.10, bf16[2,768,512]{2,1,0:T(8,128)(2,1)} %constant.2.clone.table_hbm), custom_call_target="tpu_custom_call" | custom-call | tf_op jit(solution)/shard_map/fourier/pallas_call | solution.py:89
  6.6 48.5 %all_to_all.5.received = bf16[32,192,128]{2,1,0:T(8,128)(2,1)S(1)} all-to-all(bf16[32,192,128]{2,1,0:T(8,128)(2,1)S(1)} %fourier.1), channel_id=1, replica_groups=mesh['ang'=32,'rad'=8] {'ang'}, dimensions={0} | all-to-all | bytes 3145728 | tf_op jit(solution)/shard_map/all_to_all | solution.py:273
  55.1 0.0 copy-done
  55.1 0.0 copy-start.1
  55.1 2.1 %legendre.1 = (bf16[2,512,128]{2,1,0:T(8,128)(2,1)S(1)}, bf16[2,512,128]{2,1,0:T(8,128)(2,1)S(1)}, bf16[2,512,128]{2,1,0:T(8,128)(2,1)S(1)}, bf16[2,512,128]{2,1,0:T(8,128)(2,1)S(1)}) custom-call(s32[512]{0:T(512)S(1)} %copy-done.2, bf16[16,384,512]{2,1,0:T(8,128)(2,1)S(1)} %copy-done, bf16[32,192,128]{2,1,0:T(8,128)(2,1)S(1)} %all_to_all.5.received), custom_call_target="tpu_custom_call" | custom-call | tf_op jit(solution)/shard_map/legendre/pallas_call | solution.py:160
  57.2 1.3 %collective-permute-start = (bf16[2,512,128]{2,1,0:T(8,128)(2,1)S(1)}, bf16[2,512,128]{2,1,0:T(8,128)(2,1)S(1)}, u32[]{:S(2)}, u32[]{:S(2)}) collective-permute-start(bf16[2,512,128]{2,1,0:T(8,128)(2,1)S(1)} %get-tuple-element.10), channel_id=1, source_target_pairs={{0,2},{1,3},{2,4},{3,5},{4,6},{5,7},{6,0},{7,1},{8,10},{9,11},{10,... | collective-permute-start | bytes 786440 | tf_op jit(solution)/shard_map/ppermute | solution.py:258
  58.5 2.5 %collective-permute-start.1 = (bf16[2,512,128]{2,1,0:T(8,128)(2,1)S(1)}, bf16[2,512,128]{2,1,0:T(8,128)(2,1)S(1)}, u32[]{:S(2)}, u32[]{:S(2)}) collective-permute-start(bf16[2,512,128]{2,1,0:T(8,128)(2,1)S(1)} %get-tuple-element.11), channel_id=1, source_target_pairs={{0,4},{1,5},{2,6},{3,7},{4,0},{5,1},{6,2},{7,3},{8,12},{9,13},{10,... | collective-permute-start | bytes 786440 | tf_op jit(solution)/shard_map/ppermute | solution.py:258
  61.0 4.2 %collective-permute-start.3 = (bf16[512,128]{1,0:T(8,128)(2,1)S(1)}, bf16[512,128]{1,0:T(8,128)(2,1)S(1)}, u32[]{:S(2)}, u32[]{:S(2)}) collective-permute-start(bf16[512,128]{1,0:T(8,128)(2,1)S(1)} %slice_bitcast_fusion.3), channel_id=1, source_target_pairs={{0,1},{1,0},{2,3},{3,2},{4,5},{5,4},{6,7},{7,6},{8,9},{9,8},{10,11... | collective-permute-start | bytes 393224 | tf_op jit(solution)/shard_map/ppermute | solution.py:266
  65.3 1.1 %collective-permute-start.2 = (bf16[2,512,128]{2,1,0:T(8,128)(2,1)S(1)}, bf16[2,512,128]{2,1,0:T(8,128)(2,1)S(1)}, u32[]{:S(2)}, u32[]{:S(2)}) collective-permute-start(bf16[2,512,128]{2,1,0:T(8,128)(2,1)S(1)} %get-tuple-element.12), channel_id=1, source_target_pairs={{0,6},{1,7},{2,0},{3,1},{4,2},{5,3},{6,4},{7,5},{8,14},{9,15},{10,... | collective-permute-start | bytes 786440 | tf_op jit(solution)/shard_map/ppermute | solution.py:258
  66.4 0.0 collective-permute-done.refs_1_
  66.4 4.7 %collective-permute-start.4 = (bf16[512,128]{1,0:T(8,128)(2,1)S(1)}, bf16[512,128]{1,0:T(8,128)(2,1)S(1)}, u32[]{:S(2)}, u32[]{:S(2)}) collective-permute-start(bf16[512,128]{1,0:T(8,128)(2,1)S(1)} %slice_bitcast_fusion.2), channel_id=1, source_target_pairs={{0,1},{1,0},{2,3},{3,2},{4,5},{5,4},{6,7},{7,6},{8,9},{9,8},{10,11... | collective-permute-start | bytes 393224 | tf_op jit(solution)/shard_map/ppermute | solution.py:266
  71.2 0.0 collective-permute-done.1.refs_2_
  71.2 2.8 %collective-permute-start.5 = (bf16[512,128]{1,0:T(8,128)(2,1)S(1)}, bf16[512,128]{1,0:T(8,128)(2,1)S(1)}, u32[]{:S(2)}, u32[]{:S(2)}) collective-permute-start(bf16[512,128]{1,0:T(8,128)(2,1)S(1)} %slice_bitcast_fusion.1), channel_id=1, source_target_pairs={{0,1},{1,0},{2,3},{3,2},{4,5},{5,4},{6,7},{7,6},{8,9},{9,8},{10,11... | collective-permute-start | bytes 393224 | tf_op jit(solution)/shard_map/ppermute | solution.py:266
  74.0 0.0 collective-permute-done.2.refs_3_
  74.0 1.1 %collective-permute-start.6 = (bf16[512,128]{1,0:T(8,128)(2,1)S(1)}, bf16[512,128]{1,0:T(8,128)(2,1)S(1)}, u32[]{:S(2)}, u32[]{:S(2)}) collective-permute-start(bf16[512,128]{1,0:T(8,128)(2,1)S(1)} %slice_bitcast_fusion), channel_id=1, source_target_pairs={{0,1},{1,0},{2,3},{3,2},{4,5},{5,4},{6,7},{7,6},{8,9},{9,8},{10,11... | collective-permute-start | bytes 393224 | tf_op jit(solution)/shard_map/ppermute | solution.py:266
  75.1 0.0 collective-permute-done.3.refs_4_
  75.1 0.0 collective-permute-done.4.refs_5_
  75.1 0.0 collective-permute-done.5.refs_6_
  75.1 1.0 %collective-permute-done.6.refs_7_ = bf16[512,128]{1,0:T(8,128)(2,1)S(1)} collective-permute-done((bf16[512,128]{1,0:T(8,128)(2,1)S(1)}, bf16[512,128]{1,0:T(8,128)(2,1)S(1)}, u32[]{:S(2)}, u32[]{:S(2)}) %collective-permute-start.6) | collective-permute-done | bytes 131104 | tf_op jit(solution)/shard_map/ppermute | solution.py:266
  76.1 0.0 copy-done.1
  76.1 4.3 %solve.1 = f32[64,64,128]{2,1,0:T(8,128)} custom-call(s32[512]{0:T(512)S(1)} %copy-done.2, bf16[64,128,128]{2,1,0:T(8,128)(2,1)S(1)} %copy-done.1, bf16[2,512,128]{2,1,0:T(8,128)(2,1)S(1)} %get-tuple-element.9.refs_0_, bf16[2,512,128]{2,1,0:T(8,128)(2,1)S(1)} %collective-permute-done.refs_1_, bf16[2,512,128]{2,1,0:T(8,128)(2,1)S(1)} %collective-permute-done.1.refs_2_, ...), custom_call_target="tpu_custom_call" | custom-call | tf_op jit(solution)/shard_map/solve/pallas_call | solution.py:237
  (4 shorter events, 0.0 us)
Async XLA Ops:
  0.0 0.7 copy-start.2
  0.7 54.4 %copy-start = (bf16[16,384,512]{2,1,0:T(8,128)(2,1)S(1)}, bf16[16,384,512]{2,1,0:T(8,128)(2,1)}, u32[]{:S(2)}) copy-start(bf16[16,384,512]{2,1,0:T(8,128)(2,1)} %table_ref.1) | copy-start | bytes 18874372
  55.1 21.0 %copy-start.1 = (bf16[64,128,128]{2,1,0:T(8,128)(2,1)S(1)}, bf16[64,128,128]{2,1,0:T(8,128)(2,1)}, u32[]{:S(2)}) copy-start(bf16[64,128,128]{2,1,0:T(8,128)(2,1)} %inverse_ref.1) | copy-start | bytes 6291460
  57.2 9.2 %collective-permute-start = (bf16[2,512,128]{2,1,0:T(8,128)(2,1)S(1)}, bf16[2,512,128]{2,1,0:T(8,128)(2,1)S(1)}, u32[]{:S(2)}, u32[]{:S(2)}) collective-permute-start(bf16[2,512,128]{2,1,0:T(8,128)(2,1)S(1)} %get-tuple-element.10), channel_id=1, source_target_pairs={{0,2},{1,3},{2,4},{3,5},{4,6},{5,7},{6,0},{7,1},{8,10},{9,11},{10,... | collective-permute-start | bytes 786440 | tf_op jit(solution)/shard_map/ppermute | solution.py:258
  58.5 12.7 %collective-permute-start.1 = (bf16[2,512,128]{2,1,0:T(8,128)(2,1)S(1)}, bf16[2,512,128]{2,1,0:T(8,128)(2,1)S(1)}, u32[]{:S(2)}, u32[]{:S(2)}) collective-permute-start(bf16[2,512,128]{2,1,0:T(8,128)(2,1)S(1)} %get-tuple-element.11), channel_id=1, source_target_pairs={{0,4},{1,5},{2,6},{3,7},{4,0},{5,1},{6,2},{7,3},{8,12},{9,13},{10,... | collective-permute-start | bytes 786440 | tf_op jit(solution)/shard_map/ppermute | solution.py:258
  61.0 14.1 %collective-permute-start.3 = (bf16[512,128]{1,0:T(8,128)(2,1)S(1)}, bf16[512,128]{1,0:T(8,128)(2,1)S(1)}, u32[]{:S(2)}, u32[]{:S(2)}) collective-permute-start(bf16[512,128]{1,0:T(8,128)(2,1)S(1)} %slice_bitcast_fusion.3), channel_id=1, source_target_pairs={{0,1},{1,0},{2,3},{3,2},{4,5},{5,4},{6,7},{7,6},{8,9},{9,8},{10,11... | collective-permute-start | bytes 393224 | tf_op jit(solution)/shard_map/ppermute | solution.py:266
  65.3 8.7 %collective-permute-start.2 = (bf16[2,512,128]{2,1,0:T(8,128)(2,1)S(1)}, bf16[2,512,128]{2,1,0:T(8,128)(2,1)S(1)}, u32[]{:S(2)}, u32[]{:S(2)}) collective-permute-start(bf16[2,512,128]{2,1,0:T(8,128)(2,1)S(1)} %get-tuple-element.12), channel_id=1, source_target_pairs={{0,6},{1,7},{2,0},{3,1},{4,2},{5,3},{6,4},{7,5},{8,14},{9,15},{10,... | collective-permute-start | bytes 786440 | tf_op jit(solution)/shard_map/ppermute | solution.py:258
  66.4 8.7 %collective-permute-start.4 = (bf16[512,128]{1,0:T(8,128)(2,1)S(1)}, bf16[512,128]{1,0:T(8,128)(2,1)S(1)}, u32[]{:S(2)}, u32[]{:S(2)}) collective-permute-start(bf16[512,128]{1,0:T(8,128)(2,1)S(1)} %slice_bitcast_fusion.2), channel_id=1, source_target_pairs={{0,1},{1,0},{2,3},{3,2},{4,5},{5,4},{6,7},{7,6},{8,9},{9,8},{10,11... | collective-permute-start | bytes 393224 | tf_op jit(solution)/shard_map/ppermute | solution.py:266
  71.2 3.9 %collective-permute-start.5 = (bf16[512,128]{1,0:T(8,128)(2,1)S(1)}, bf16[512,128]{1,0:T(8,128)(2,1)S(1)}, u32[]{:S(2)}, u32[]{:S(2)}) collective-permute-start(bf16[512,128]{1,0:T(8,128)(2,1)S(1)} %slice_bitcast_fusion.1), channel_id=1, source_target_pairs={{0,1},{1,0},{2,3},{3,2},{4,5},{5,4},{6,7},{7,6},{8,9},{9,8},{10,11... | collective-permute-start | bytes 393224 | tf_op jit(solution)/shard_map/ppermute | solution.py:266
  74.0 2.1 %collective-permute-start.6 = (bf16[512,128]{1,0:T(8,128)(2,1)S(1)}, bf16[512,128]{1,0:T(8,128)(2,1)S(1)}, u32[]{:S(2)}, u32[]{:S(2)}) collective-permute-start(bf16[512,128]{1,0:T(8,128)(2,1)S(1)} %slice_bitcast_fusion), channel_id=1, source_target_pairs={{0,1},{1,0},{2,3},{3,2},{4,5},{5,4},{6,7},{7,6},{8,9},{9,8},{10,11... | collective-permute-start | bytes 393224 | tf_op jit(solution)/shard_map/ppermute | solution.py:266

commit v4 on v3

v4 whole, which is shorter than its diff:
```python
import functools
import math

import jax
import jax.numpy as jnp
import numpy as np
from jax import lax
from jax.experimental import pallas as pl
from jax.experimental.pallas import tpu as pltpu
from jax.sharding import PartitionSpec as P

LONS = 1536
HALF_LONS = LONS // 2
ORDERS = 512
PAIRS = ORDERS // 2
NA, NR = 32, 8
NX, NC = 4, 2
ARRIVALS = (0, 2, 1, 3)
DIRECT = (1, 3)
F32 = jnp.float32
BF16 = jnp.bfloat16
SMEM = pl.BlockSpec(memory_space=pltpu.SMEM)
VMEM = pl.BlockSpec(memory_space=pltpu.VMEM)
HBM = pl.BlockSpec(memory_space=pltpu.HBM)
PARAMS = pltpu.CompilerParams(vmem_limit_bytes=24 * 2**20)
ROWS = 256
LINE = 72


def transform_tables():
    longitude = np.arange(HALF_LONS, dtype=np.int64)[:, None]
    halves = []
    for pairs in np.split(np.arange(PAIRS, dtype=np.int64), 2):
        tables = []
        for order in (2 * pairs, ORDERS - 1 - 2 * pairs):
            angle = (longitude * order[None, :] % LONS) * (2.0 * math.pi / LONS)
            columns = np.concatenate([np.cos(angle), -np.sin(angle)], axis=1)
            tables.append((columns / math.sqrt(LONS)).astype(np.float32).astype(BF16))
        halves.append(np.stack(tables))
    return np.stack(halves)


def fourier_kernel(lats, order_hbm, x_hbm, table_hbm, out_ref, order_ref, x_ref, table_ref, mixed, low, high, turned, sems):
    place = lax.axis_index("ang")
    rows = x_ref.shape[0]
    columns = rows // lats
    pairs = PAIRS // NA
    starts = range(0, rows, ROWS)
    order_copy = pltpu.make_async_copy(order_hbm, order_ref, sems.at[0])
    x_copies = [
        pltpu.make_async_copy(x_hbm.at[pl.ds(start, ROWS)], x_ref.at[pl.ds(start, ROWS)], sems.at[1 + index])
        for index, start in enumerate(starts)
    ]
    table_copies = [
        [
            pltpu.make_async_copy(table_hbm.at[half, parity], table_ref.at[half, parity], sems.at[4 + half * 2 + parity])
            for parity in range(2)
        ]
        for half in range(2)
    ]
    for copy in (x_copies[0], *table_copies[0], *x_copies[1:], *table_copies[1], order_copy):
        copy.start()

    def turn(half, product, row):
        placed = jnp.where(place >= NA // 2, lats - 1 - row, row)
        picked = [product[part, pl.ds(row, columns, stride=lats), :] for part in range(4)]
        block = jnp.concatenate(picked, axis=0).T
        turned[pl.ds(half * 128 * lats + placed, 128, stride=lats), :] = block

    for index, start in enumerate(starts):
        x_copies[index].wait()
        near = x_ref[start : start + ROWS, :HALF_LONS].astype(F32)
        far = x_ref[start : start + ROWS, HALF_LONS:].astype(F32)
        mixed[0, start : start + ROWS, :] = (near + far).astype(BF16)
        mixed[1, start : start + ROWS, :] = (near - far).astype(BF16)
        for parity in range(2):
            if start == 0:
                table_copies[0][parity].wait()
            result = jnp.dot(mixed[parity, start : start + ROWS, :], table_ref[0, parity], preferred_element_type=F32)
            for part in range(2):
                low[parity * 2 + part, start : start + ROWS, :] = result[:, part * 128 : part * 128 + 128]
    for parity in range(2):
        table_copies[1][parity].wait()
    share = lats // 2
    for index in range(2):
        result = jnp.dot(mixed[index], table_ref[1, index], preferred_element_type=F32)
        for part in range(2):
            high[index * 2 + part] = result[:, part * 128 : part * 128 + 128]
        for row in range(index * share, (index + 1) * share):
            turn(0, low, row)

    def turn_high(row, _):
        turn(1, high, row)
        return 0

    lax.fori_loop(0, lats, turn_high, 0, unroll=8)
    order_copy.wait()

    def put(device, _):
        for local in range(0, pairs, 2):
            picked = []
            for offset in range(2):
                order = order_ref[(device * pairs + local + offset) * 2]
                pair = lax.shift_right_logical(order ^ ((order & 1) * (ORDERS - 1)), 1)
                picked.append(turned[pl.ds(pl.multiple_of(pair * lats, 8), lats), :])
            out_ref[device, local * lats : (local + 2) * lats, :] = jnp.concatenate(picked, axis=0).astype(BF16)
        return 0

    lax.fori_loop(0, NA, put, 0, unroll=2)


def fourier_stage(slot_order, rows, lats):
    table = transform_tables()
    count = rows.shape[0]
    return pl.pallas_call(
        functools.partial(fourier_kernel, lats),
        out_shape=jax.ShapeDtypeStruct((NA, PAIRS // NA * lats, 128), BF16),
        in_specs=[HBM, HBM, HBM],
        out_specs=VMEM,
        scratch_shapes=[
            pltpu.SMEM(slot_order.shape, jnp.int32),
            pltpu.VMEM(rows.shape, BF16),
            pltpu.VMEM(table.shape, BF16),
            pltpu.VMEM((2, count, HALF_LONS), BF16),
            pltpu.VMEM((4, count, 128), F32),
            pltpu.VMEM((4, count, 128), F32),
            pltpu.VMEM((PAIRS * lats, 128), F32),
            pltpu.SemaphoreType.DMA((8,)),
        ],
        compiler_params=pltpu.CompilerParams(vmem_limit_bytes=52 * 2**20),
        name="fourier",
    )(slot_order, rows, jnp.asarray(table))


def legendre_kernel(lats, order_ref, table_ref, received, *refs):
    outs, (sent, symmetric, antisymmetric) = refs[:-3], refs[-3:]
    place = lax.axis_index("ang")
    column = lax.axis_index("rad")
    here_x, here_c = column // NC, column % NC
    slots, _, degrees = table_ref.shape
    half = NA // 2
    degree = lax.broadcasted_iota(jnp.int32, (64, degrees), 1)

    def upper_first(pair):
        return lax.shift_right_logical(order_ref[place * slots + pair * 2], 8)

    for step in range(slots // 4):
        at = slice(step * 2 * lats, (step + 1) * 2 * lats)
        pieces = [received[source, at, :].astype(F32) for source in range(2 * half)]
        for pair in range(step * 2, step * 2 + 2):
            rows = slice(pair % 2 * lats, (pair % 2 + 1) * lats)
            north = jnp.concatenate([piece[rows] for piece in pieces[:half]], axis=0)
            mirrored = jnp.concatenate([piece[rows] for piece in pieces[half:][::-1]], axis=0)
            symmetric[pair] = (north + mirrored).astype(BF16).T
            antisymmetric[pair] = (north - mirrored).astype(BF16).T

    for pair in range(slots // 2):
        first = order_ref[place * slots + pair * 2]
        lower = jnp.where(first >= ORDERS // 2, ORDERS - 1 - first, first)
        chosen = []
        for which, order in enumerate((lower, ORDERS - 1 - lower)):
            begin = which * (degrees // 2)
            wanted = pl.ds(pl.multiple_of((order & 1) * 64, 64), 64)
            both = jnp.concatenate([symmetric[pair, wanted], antisymmetric[pair, wanted]], axis=0)
            result = jnp.dot(both, table_ref[pair * 2 + (upper_first(pair) ^ which), :, begin:], preferred_element_type=F32)
            here = degree[:, begin:]
            kept = jnp.where(((here ^ order) & 1) == 0, result[:64], result[64:])
            chosen.append(jnp.where(here >= order, kept, 0.0).astype(BF16))
        out_at = slice(pair * 64, pair * 64 + 64)
        for block in range(NR):
            left = chosen[0][:, block * 64 : block * 64 + 64]
            right = jnp.zeros_like(left)
            if block * 64 >= degrees // 2:
                right = chosen[1][:, block * 64 - degrees // 2 : block * 64 - degrees // 2 + 64]
            step_x = (block // NC - here_x) & (NX - 1)
            sent[step_x * NC + ((block % NC) ^ here_c), out_at, :] = jnp.concatenate([left, right], axis=1)
    outs = iter(outs)
    for step_x in range(NX):
        if step_x in DIRECT:
            for step_c in range(NC):
                next(outs)[...] = sent[step_x * NC + step_c]
        else:
            next(outs)[...] = sent[step_x * NC : step_x * NC + NC]


def legendre_stage(slot_order, received, legendre, lats):
    slots, _, _ = legendre.shape
    rows = slots * 32
    shapes = []
    for step_x in range(NX):
        if step_x in DIRECT:
            shapes += [jax.ShapeDtypeStruct((rows, 128), BF16)] * NC
        else:
            shapes.append(jax.ShapeDtypeStruct((NC, rows, 128), BF16))
    sent = pl.pallas_call(
        functools.partial(legendre_kernel, lats),
        out_shape=shapes,
        in_specs=[SMEM, VMEM, VMEM],
        out_specs=[VMEM] * len(shapes),
        scratch_shapes=[
            pltpu.VMEM((NR, slots * 32, 128), BF16),
            pltpu.VMEM((slots // 2, 128, legendre.shape[1]), BF16),
            pltpu.VMEM((slots // 2, 128, legendre.shape[1]), BF16),
        ],
        compiler_params=pltpu.CompilerParams(vmem_limit_bytes=24 * 2**20),
        name="legendre",
    )(slot_order, legendre, received)
    return sent


def solve_kernel(order_ref, inverse_ref, *refs):
    mine, others, (out_hbm, received, turned, solved, sems) = refs[:NX], refs[NX : 2 * NX], refs[-5:]
    place = lax.axis_index("ang")
    column = lax.axis_index("rad")
    here_x, here_c = column // NC, column % NC
    degrees = inverse_ref.shape[0]
    lines = solved.shape[1]
    pairs = lines // 8
    for index, step_x in enumerate(ARRIVALS):
        source = ((here_x - step_x) & (NX - 1)) * NC + here_c
        received[source] = mine[index][...] if step_x in DIRECT else mine[index][0]
        received[source ^ 1] = others[index][...]
    for pair in range(pairs):
        upper_first = lax.shift_right_logical(order_ref[(place * pairs + pair) * 2], 8)
        for part in range(4):
            at = slice(pair * 64 + part * 16, pair * 64 + part * 16 + 16)
            block = jnp.concatenate([received[source, at, :] for source in range(NR)], axis=0)
            block = block.astype(F32).T
            for which in range(2):
                slot = pair * 2 + (upper_first ^ which)
                line = (part // 2) * (4 * pairs) + slot * 2 + part % 2
                turned[pl.ds(pl.multiple_of(line * LINE, 8), 64), :] = block[which * 64 : which * 64 + 64]

    def copy(group):
        at = pl.ds(pl.multiple_of(group * 8, 8), 8)
        return pltpu.make_async_copy(solved.at[group], out_hbm.at[:, at], sems.at[group])

    def solve(group, _):
        for degree in range(8):
            picked = turned[pl.ds(group * 8 + degree, lines, stride=LINE), :].astype(BF16)
            solved[group, :, degree, :] = lax.dot_general(
                picked, inverse_ref[group * 8 + degree], (((1,), (1,)), ((), ())), preferred_element_type=F32
            )
        copy(group).start()
        return 0

    lax.fori_loop(0, degrees // 8, solve, 0, unroll=8)
    for group in range(degrees // 8):
        copy(group).wait()


def solve_stage(slot_order, mine, others, inverses):
    degrees = inverses.shape[0]
    lines = others[0].shape[0] // 8
    operands = [slot_order, inverses, *(mine[i] for i in ARRIVALS), *(others[i] for i in ARRIVALS)]
    return pl.pallas_call(
        solve_kernel,
        out_shape=jax.ShapeDtypeStruct((lines, degrees, 128), F32),
        in_specs=[SMEM] + [VMEM] * (len(operands) - 1),
        out_specs=HBM,
        scratch_shapes=[
            pltpu.VMEM((NR, lines * 8, 128), BF16),
            pltpu.VMEM((lines * LINE, 128), F32),
            pltpu.VMEM((degrees // 8, lines, 8, 128), F32),
            pltpu.SemaphoreType.DMA((degrees // 8,)),
        ],
        compiler_params=PARAMS,
        name="solve",
    )(*operands)


def along_rad(sent):
    def move(part, step_x, step_c):
        pairs = [(a, (a // NC + step_x) % NX * NC + (a % NC ^ step_c)) for a in range(NX * NC)]
        return lax.ppermute(part, "rad", pairs)

    sent = iter(sent)
    mine, others = [], []
    for step_x in range(NX):
        part = next(sent)
        if step_x in DIRECT:
            mine.append(move(part, step_x, 0))
            others.append(move(next(sent), step_x, 1))
        else:
            mine.append(move(part, step_x, 0) if step_x else part)
            others.append(move(mine[-1][1], 0, 1))
    return mine, others


def body(grid_field, slot_order, legendre, inverses):
    fields, radii, lats, lons = grid_field.shape
    slots = legendre.shape[0]
    sent = fourier_stage(slot_order, grid_field.reshape(fields * radii * lats, lons), lats)
    received = lax.all_to_all(sent, "ang", split_axis=0, concat_axis=0)
    mine, others = along_rad(legendre_stage(slot_order, received, legendre, lats))
    spectrum = solve_stage(slot_order, mine, others, inverses)
    return spectrum.reshape(2, slots, fields, inverses.shape[0], 128)


def solution(mesh):
    placed = (P(None, "rad", "ang", None), P(), P("ang", None, None), P("rad", None, None))
    return jax.shard_map(
        body,
        mesh=mesh,
        in_specs=placed,
        out_specs=P(None, "ang", None, "rad", None),
        check_vma=False,
    )
```

time: 80.8 us -> 77.9 us (0.964)
  starting transfers between devices: 17.8 us -> 15.4 us
  Pallas kernels: 12.3 us -> 10.8 us
  waiting for transfers between devices: 0.99 us -> 2.1 us
    ppermute x7, starting transfers between devices: 17.8 us -> 15.4 us  [move(): return lax.ppermute(part, 'rad', pairs)]
    ppermute x7, waiting for transfers between devices: 0.99 us -> 2.1 us  [move(): return lax.ppermute(part, 'rad', pairs)]
  transfers between devices with their start and end apart: 7 -> 7, of which waited for: 1 -> 2; matrix products, arithmetic and copies ran while one was open for 0% -> 0% of each run, Pallas kernels for 0% -> 0%
where the time goes in v4:
time: 77.9 us; the launch traced here: 77.6 us
  blocking collectives  48.5 us (62%)
  starting transfers between devices  15.4 us (20%)
  Pallas kernels  10.8 us (14%)
  waiting for transfers between devices  2.1 us (3%)
    all_to_all x1, blocking collectives, body(): received = lax.all_to_all(sent, 'ang', split_axis=0, concat_axis=0)  48.5 us
    ppermute x7, starting transfers between devices, move(): return lax.ppermute(part, 'rad', pairs)  15.4 us
    pallas_call x1, Pallas kernels, fourier_stage(): pl.pallas_call(functools.partial(fourier_kernel, lats), out_shape=jax.Sha...  5.16 us
    pallas_call x1, Pallas kernels, solve_stage(): pl.pallas_call(solve_kernel, out_shape=jax.ShapeDtypeStruct((lines, degre...  3.56 us
    pallas_call x1, Pallas kernels, legendre_stage(): pl.pallas_call(functools.partial(legendre_kernel, lats), out_shape=shapes...  2.11 us
    ppermute x7, waiting for transfers between devices, move(): return lax.ppermute(part, 'rad', pairs)  2.1 us
  transfers between devices with their start and end apart: 7, of which 2 were waited for; matrix products, arithmetic and copies ran while one was open for 0% of the time, Pallas kernels for 0%

profile of v4, /device:TPU:1, one launch (start us, length us, event | category | flops | bytes accessed | tf_op | source)
XLA Modules:
  0.0 77.6 jit_solution(16506440388254268674)
XLA Ops:
  0.0 0.0 copy-start.2
  0.0 0.7 copy-done.2
  0.7 0.0 copy-start
  0.7 5.2 %fourier.1 = bf16[32,192,128]{2,1,0:T(8,128)(2,1)S(1)} custom-call(s32[512]{0:T(512)S(1)} %copy-done.2, bf16[768,1536]{1,0:T(8,128)(2,1)} %bitcast.6, bf16[2,2,768,256]{3,2,1,0:T(8,128)(2,1)} %constant.2.clone.table_hbm), custom_call_target="tpu_custom_call" | custom-call | tf_op jit(solution)/shard_map/fourier/pallas_call | solution.py:115
  5.8 48.5 %all_to_all.5.received = bf16[32,192,128]{2,1,0:T(8,128)(2,1)S(1)} all-to-all(bf16[32,192,128]{2,1,0:T(8,128)(2,1)S(1)} %fourier.1), channel_id=1, replica_groups=mesh['ang'=32,'rad'=8] {'ang'}, dimensions={0} | all-to-all | bytes 3145728 | tf_op jit(solution)/shard_map/all_to_all | solution.py:294
  54.4 0.0 copy-done
  54.4 0.0 copy-start.1
  54.4 2.1 %legendre.1 = (bf16[2,512,128]{2,1,0:T(8,128)(2,1)S(1)}, bf16[512,128]{1,0:T(8,128)(2,1)S(1)}, bf16[512,128]{1,0:T(8,128)(2,1)S(1)}, bf16[2,512,128]{2,1,0:T(8,1...) custom-call(s32[512]{0:T(512)S(1)} %copy-done.2, bf16[16,384,512]{2,1,0:T(8,128)(2,1)S(1)} %copy-done, ...), custom_call_target="tpu_custom_call" | custom-call | tf_op jit(solution)/shard_map/legendre/pallas_call | solution.py:195
  56.5 2.8 %collective-permute-start = (bf16[2,512,128]{2,1,0:T(8,128)(2,1)S(1)}, bf16[2,512,128]{2,1,0:T(8,128)(2,1)S(1)}, u32[]{:S(2)}, u32[]{:S(2)}) collective-permute-start(bf16[2,512,128]{2,1,0:T(8,128)(2,1)S(1)} %get-tuple-element.12), channel_id=1, source_target_pairs={{0,4},{1,5},{2,6},{3,7},{4,0},{5,1},{6,2},{7,3},{8,12},{9,13},{10,... | collective-permute-start | bytes 786440 | tf_op jit(solution)/shard_map/ppermute | solution.py:275
  59.3 4.0 %collective-permute-start.3 = (bf16[512,128]{1,0:T(8,128)(2,1)S(1)}, bf16[512,128]{1,0:T(8,128)(2,1)S(1)}, u32[]{:S(2)}, u32[]{:S(2)}) collective-permute-start(bf16[512,128]{1,0:T(8,128)(2,1)S(1)} %slice_bitcast_fusion.1), channel_id=1, source_target_pairs={{0,1},{1,0},{2,3},{3,2},{4,5},{5,4},{6,7},{7,6},{8,9},{9,8},{10,11... | collective-permute-start | bytes 393224 | tf_op jit(solution)/shard_map/ppermute | solution.py:275
  63.3 0.3 collective-permute-start.1
  63.6 2.4 %collective-permute-start.2 = (bf16[512,128]{1,0:T(8,128)(2,1)S(1)}, bf16[512,128]{1,0:T(8,128)(2,1)S(1)}, u32[]{:S(2)}, u32[]{:S(2)}) collective-permute-start(bf16[512,128]{1,0:T(8,128)(2,1)S(1)} %get-tuple-element.14), channel_id=1, source_target_pairs={{0,6},{1,7},{2,0},{3,1},{4,2},{5,3},{6,4},{7,5},{8,14},{9,15},{10,... | collective-permute-start | bytes 393224 | tf_op jit(solution)/shard_map/ppermute | solution.py:275
  66.0 0.0 collective-permute-start.5
  66.0 0.0 collective-permute-done.refs_1_
  66.0 5.8 %collective-permute-start.6 = (bf16[512,128]{1,0:T(8,128)(2,1)S(1)}, bf16[512,128]{1,0:T(8,128)(2,1)S(1)}, u32[]{:S(2)}, u32[]{:S(2)}) collective-permute-start(bf16[512,128]{1,0:T(8,128)(2,1)S(1)} %get-tuple-element.16), channel_id=1, source_target_pairs={{0,7},{1,6},{2,1},{3,0},{4,3},{5,2},{6,5},{7,4},{8,15},{9,14},{10,... | collective-permute-start | bytes 393224 | tf_op jit(solution)/shard_map/ppermute | solution.py:275
  71.8 0.0 collective-permute-done.3.refs_4_
  71.8 0.1 collective-permute-start.4
  71.9 0.0 collective-permute-done.1.refs_2_
  71.9 0.0 collective-permute-done.2.refs_3_
  71.9 1.4 %collective-permute-done.5.refs_6_ = bf16[512,128]{1,0:T(8,128)(2,1)S(1)} collective-permute-done((bf16[512,128]{1,0:T(8,128)(2,1)S(1)}, bf16[512,128]{1,0:T(8,128)(2,1)S(1)}, u32[]{:S(2)}, u32[]{:S(2)}) %collective-permute-start.5) | collective-permute-done | bytes 131104 | tf_op jit(solution)/shard_map/ppermute | solution.py:275
  73.3 0.7 collective-permute-done.6.refs_7_
  74.0 0.0 collective-permute-done.4.refs_5_
  74.0 0.0 copy-done.1
  74.0 3.6 %solve.1 = f32[64,64,128]{2,1,0:T(8,128)} custom-call(s32[512]{0:T(512)S(1)} %copy-done.2, bf16[64,128,128]{2,1,0:T(8,128)(2,1)S(1)} %copy-done.1, bf16[2,512,128]{2,1,0:T(8,128)(2,1)S(1)} %get-tuple-element.11.refs_0_, bf16[2,512,128]{2,1,0:T(8,128)(2,1)S(1)} %collective-permute-done.refs_1_, bf16[512,128]{1,0:T(8,128)(2,1)S(1)} %collective-permute-done.1.refs_2_, ...), custom_call_target="tpu_custom_call" | custom-call | tf_op jit(solution)/shard_map/solve/pallas_call | solution.py:256
  (2 shorter events, 0.0 us)
Async XLA Ops:
  0.0 0.7 copy-start.2
  0.7 53.7 %copy-start = (bf16[16,384,512]{2,1,0:T(8,128)(2,1)S(1)}, bf16[16,384,512]{2,1,0:T(8,128)(2,1)}, u32[]{:S(2)}) copy-start(bf16[16,384,512]{2,1,0:T(8,128)(2,1)} %table_ref.1) | copy-start | bytes 18874372
  54.4 19.7 %copy-start.1 = (bf16[64,128,128]{2,1,0:T(8,128)(2,1)S(1)}, bf16[64,128,128]{2,1,0:T(8,128)(2,1)}, u32[]{:S(2)}) copy-start(bf16[64,128,128]{2,1,0:T(8,128)(2,1)} %inverse_ref.1) | copy-start | bytes 6291460
  56.5 9.5 %collective-permute-start = (bf16[2,512,128]{2,1,0:T(8,128)(2,1)S(1)}, bf16[2,512,128]{2,1,0:T(8,128)(2,1)S(1)}, u32[]{:S(2)}, u32[]{:S(2)}) collective-permute-start(bf16[2,512,128]{2,1,0:T(8,128)(2,1)S(1)} %get-tuple-element.12), channel_id=1, source_target_pairs={{0,4},{1,5},{2,6},{3,7},{4,0},{5,1},{6,2},{7,3},{8,12},{9,13},{10,... | collective-permute-start | bytes 786440 | tf_op jit(solution)/shard_map/ppermute | solution.py:275
  59.3 12.5 %collective-permute-start.3 = (bf16[512,128]{1,0:T(8,128)(2,1)S(1)}, bf16[512,128]{1,0:T(8,128)(2,1)S(1)}, u32[]{:S(2)}, u32[]{:S(2)}) collective-permute-start(bf16[512,128]{1,0:T(8,128)(2,1)S(1)} %slice_bitcast_fusion.1), channel_id=1, source_target_pairs={{0,1},{1,0},{2,3},{3,2},{4,5},{5,4},{6,7},{7,6},{8,9},{9,8},{10,11... | collective-permute-start | bytes 393224 | tf_op jit(solution)/shard_map/ppermute | solution.py:275
  63.3 8.6 %collective-permute-start.1 = (bf16[512,128]{1,0:T(8,128)(2,1)S(1)}, bf16[512,128]{1,0:T(8,128)(2,1)S(1)}, u32[]{:S(2)}, u32[]{:S(2)}) collective-permute-start(bf16[512,128]{1,0:T(8,128)(2,1)S(1)} %get-tuple-element.13), channel_id=1, source_target_pairs={{0,2},{1,3},{2,4},{3,5},{4,6},{5,7},{6,0},{7,1},{8,10},{9,11},{10,... | collective-permute-start | bytes 393224 | tf_op jit(solution)/shard_map/ppermute | solution.py:275
  63.6 8.3 %collective-permute-start.2 = (bf16[512,128]{1,0:T(8,128)(2,1)S(1)}, bf16[512,128]{1,0:T(8,128)(2,1)S(1)}, u32[]{:S(2)}, u32[]{:S(2)}) collective-permute-start(bf16[512,128]{1,0:T(8,128)(2,1)S(1)} %get-tuple-element.14), channel_id=1, source_target_pairs={{0,6},{1,7},{2,0},{3,1},{4,2},{5,3},{6,4},{7,5},{8,14},{9,15},{10,... | collective-permute-start | bytes 393224 | tf_op jit(solution)/shard_map/ppermute | solution.py:275
  66.0 7.3 %collective-permute-start.5 = (bf16[512,128]{1,0:T(8,128)(2,1)S(1)}, bf16[512,128]{1,0:T(8,128)(2,1)S(1)}, u32[]{:S(2)}, u32[]{:S(2)}) collective-permute-start(bf16[512,128]{1,0:T(8,128)(2,1)S(1)} %get-tuple-element.15), channel_id=1, source_target_pairs={{0,3},{1,2},{2,5},{3,4},{4,7},{5,6},{6,1},{7,0},{8,11},{9,10},{10,... | collective-permute-start | bytes 393224 | tf_op jit(solution)/shard_map/ppermute | solution.py:275
  66.0 8.0 %collective-permute-start.6 = (bf16[512,128]{1,0:T(8,128)(2,1)S(1)}, bf16[512,128]{1,0:T(8,128)(2,1)S(1)}, u32[]{:S(2)}, u32[]{:S(2)}) collective-permute-start(bf16[512,128]{1,0:T(8,128)(2,1)S(1)} %get-tuple-element.16), channel_id=1, source_target_pairs={{0,7},{1,6},{2,1},{3,0},{4,3},{5,2},{6,5},{7,4},{8,15},{9,14},{10,... | collective-permute-start | bytes 393224 | tf_op jit(solution)/shard_map/ppermute | solution.py:275
  71.8 2.2 %collective-permute-start.4 = (bf16[512,128]{1,0:T(8,128)(2,1)S(1)}, bf16[512,128]{1,0:T(8,128)(2,1)S(1)}, u32[]{:S(2)}, u32[]{:S(2)}) collective-permute-start(bf16[512,128]{1,0:T(8,128)(2,1)S(1)} %slice_bitcast_fusion), channel_id=1, source_target_pairs={{0,1},{1,0},{2,3},{3,2},{4,5},{5,4},{6,7},{7,6},{8,9},{9,8},{10,11... | collective-permute-start | bytes 393224 | tf_op jit(solution)/shard_map/ppermute | solution.py:275

commit v5 on v4

--- a/solution.py
+++ b/solution.py
@@ -23,7 +23,7 @@
 VMEM = pl.BlockSpec(memory_space=pltpu.VMEM)
 HBM = pl.BlockSpec(memory_space=pltpu.HBM)
 PARAMS = pltpu.CompilerParams(vmem_limit_bytes=24 * 2**20)
-ROWS = 256
+CUTS = ((0, 128), (128, 384), (384, 768))
 LINE = 72
 
 
@@ -42,14 +42,12 @@
 
 def fourier_kernel(lats, order_hbm, x_hbm, table_hbm, out_ref, order_ref, x_ref, table_ref, mixed, low, high, turned, sems):
     place = lax.axis_index("ang")
-    rows = x_ref.shape[0]
-    columns = rows // lats
+    columns = x_ref.shape[0] // lats
     pairs = PAIRS // NA
-    starts = range(0, rows, ROWS)
     order_copy = pltpu.make_async_copy(order_hbm, order_ref, sems.at[0])
     x_copies = [
-        pltpu.make_async_copy(x_hbm.at[pl.ds(start, ROWS)], x_ref.at[pl.ds(start, ROWS)], sems.at[1 + index])
-        for index, start in enumerate(starts)
+        pltpu.make_async_copy(x_hbm.at[start:stop], x_ref.at[start:stop], sems.at[1 + index])
+        for index, (start, stop) in enumerate(CUTS)
     ]
     table_copies = [
         [
@@ -67,18 +65,18 @@
         block = jnp.concatenate(picked, axis=0).T
         turned[pl.ds(half * 128 * lats + placed, 128, stride=lats), :] = block
 
-    for index, start in enumerate(starts):
+    for index, (start, stop) in enumerate(CUTS):
         x_copies[index].wait()
-        near = x_ref[start : start + ROWS, :HALF_LONS].astype(F32)
-        far = x_ref[start : start + ROWS, HALF_LONS:].astype(F32)
-        mixed[0, start : start + ROWS, :] = (near + far).astype(BF16)
-        mixed[1, start : start + ROWS, :] = (near - far).astype(BF16)
+        near = x_ref[start:stop, :HALF_LONS].astype(F32)
+        far = x_ref[start:stop, HALF_LONS:].astype(F32)
+        mixed[0, start:stop, :] = (near + far).astype(BF16)
+        mixed[1, start:stop, :] = (near - far).astype(BF16)
         for parity in range(2):
             if start == 0:
                 table_copies[0][parity].wait()
-            result = jnp.dot(mixed[parity, start : start + ROWS, :], table_ref[0, parity], preferred_element_type=F32)
+            result = jnp.dot(mixed[parity, start:stop, :], table_ref[0, parity], preferred_element_type=F32)
             for part in range(2):
-                low[parity * 2 + part, start : start + ROWS, :] = result[:, part * 128 : part * 128 + 128]
+                low[parity * 2 + part, start:stop, :] = result[:, part * 128 : part * 128 + 128]
     for parity in range(2):
         table_copies[1][parity].wait()
     share = lats // 2
@@ -93,7 +91,7 @@
         turn(1, high, row)
         return 0
 
-    lax.fori_loop(0, lats, turn_high, 0, unroll=8)
+    lax.fori_loop(0, lats, turn_high, 0, unroll=24)
     order_copy.wait()
 
     def put(device, _):
@@ -106,7 +104,7 @@
             out_ref[device, local * lats : (local + 2) * lats, :] = jnp.concatenate(picked, axis=0).astype(BF16)
         return 0
 
-    lax.fori_loop(0, NA, put, 0, unroll=2)
+    lax.fori_loop(0, NA, put, 0, unroll=8)
 
 
 def fourier_stage(slot_order, rows, lats):
@@ -225,7 +223,7 @@
         for part in range(4):
             at = slice(pair * 64 + part * 16, pair * 64 + part * 16 + 16)
             block = jnp.concatenate([received[source, at, :] for source in range(NR)], axis=0)
-            block = block.astype(F32).T
+            block = block.T.astype(F32)
             for which in range(2):
                 slot = pair * 2 + (upper_first ^ which)
                 line = (part // 2) * (4 * pairs) + slot * 2 + part % 2

time: 77.9 us -> 77.2 us (level)
  no operation moved by 1% of the time
where the time goes in v5:
time: 77.2 us; the launch traced here: 76.9 us
  blocking collectives  48.5 us (63%)
  starting transfers between devices  15.4 us (20%)
  Pallas kernels  10.2 us (13%)
  waiting for transfers between devices  2.11 us (3%)
    all_to_all x1, blocking collectives, body(): received = lax.all_to_all(sent, 'ang', split_axis=0, concat_axis=0)  48.5 us
    ppermute x7, starting transfers between devices, move(): return lax.ppermute(part, 'rad', pairs)  15.4 us
    pallas_call x1, Pallas kernels, fourier_stage(): pl.pallas_call(functools.partial(fourier_kernel, lats), out_shape=jax.Sha...  4.55 us
    pallas_call x1, Pallas kernels, solve_stage(): pl.pallas_call(solve_kernel, out_shape=jax.ShapeDtypeStruct((lines, degre...  3.51 us
    pallas_call x1, Pallas kernels, legendre_stage(): pl.pallas_call(functools.partial(legendre_kernel, lats), out_shape=shapes...  2.11 us
    ppermute x7, waiting for transfers between devices, move(): return lax.ppermute(part, 'rad', pairs)  2.11 us
  transfers between devices with their start and end apart: 7, of which 2 were waited for; matrix products, arithmetic and copies ran while one was open for 0% of the time, Pallas kernels for 0%

profile of v5, /device:TPU:1, one launch (start us, length us, event | category | flops | bytes accessed | tf_op | source)
XLA Modules:
  0.0 76.9 jit_solution(18132152238814951221)
XLA Ops:
  0.0 0.0 copy-start.2
  0.0 0.7 copy-done.2
  0.7 0.0 copy-start
  0.7 4.5 %fourier.1 = bf16[32,192,128]{2,1,0:T(8,128)(2,1)S(1)} custom-call(s32[512]{0:T(512)S(1)} %copy-done.2, bf16[768,1536]{1,0:T(8,128)(2,1)} %bitcast.6, bf16[2,2,768,256]{3,2,1,0:T(8,128)(2,1)} %constant.2.clone.table_hbm), custom_call_target="tpu_custom_call" | custom-call | tf_op jit(solution)/shard_map/fourier/pallas_call | solution.py:113
  5.2 48.5 %all_to_all.5.received = bf16[32,192,128]{2,1,0:T(8,128)(2,1)S(1)} all-to-all(bf16[32,192,128]{2,1,0:T(8,128)(2,1)S(1)} %fourier.1), channel_id=1, replica_groups=mesh['ang'=32,'rad'=8] {'ang'}, dimensions={0} | all-to-all | bytes 3145728 | tf_op jit(solution)/shard_map/all_to_all | solution.py:292
  53.7 0.0 copy-done
  53.7 0.0 copy-start.1
  53.7 2.1 %legendre.1 = (bf16[2,512,128]{2,1,0:T(8,128)(2,1)S(1)}, bf16[512,128]{1,0:T(8,128)(2,1)S(1)}, bf16[512,128]{1,0:T(8,128)(2,1)S(1)}, bf16[2,512,128]{2,1,0:T(8,1...) custom-call(s32[512]{0:T(512)S(1)} %copy-done.2, bf16[16,384,512]{2,1,0:T(8,128)(2,1)S(1)} %copy-done, ...), custom_call_target="tpu_custom_call" | custom-call | tf_op jit(solution)/shard_map/legendre/pallas_call | solution.py:193
  55.9 2.8 %collective-permute-start = (bf16[2,512,128]{2,1,0:T(8,128)(2,1)S(1)}, bf16[2,512,128]{2,1,0:T(8,128)(2,1)S(1)}, u32[]{:S(2)}, u32[]{:S(2)}) collective-permute-start(bf16[2,512,128]{2,1,0:T(8,128)(2,1)S(1)} %get-tuple-element.12), channel_id=1, source_target_pairs={{0,4},{1,5},{2,6},{3,7},{4,0},{5,1},{6,2},{7,3},{8,12},{9,13},{10,... | collective-permute-start | bytes 786440 | tf_op jit(solution)/shard_map/ppermute | solution.py:273
  58.7 4.0 %collective-permute-start.3 = (bf16[512,128]{1,0:T(8,128)(2,1)S(1)}, bf16[512,128]{1,0:T(8,128)(2,1)S(1)}, u32[]{:S(2)}, u32[]{:S(2)}) collective-permute-start(bf16[512,128]{1,0:T(8,128)(2,1)S(1)} %slice_bitcast_fusion.1), channel_id=1, source_target_pairs={{0,1},{1,0},{2,3},{3,2},{4,5},{5,4},{6,7},{7,6},{8,9},{9,8},{10,11... | collective-permute-start | bytes 393224 | tf_op jit(solution)/shard_map/ppermute | solution.py:273
  62.7 0.3 collective-permute-start.1
  63.0 2.4 %collective-permute-start.2 = (bf16[512,128]{1,0:T(8,128)(2,1)S(1)}, bf16[512,128]{1,0:T(8,128)(2,1)S(1)}, u32[]{:S(2)}, u32[]{:S(2)}) collective-permute-start(bf16[512,128]{1,0:T(8,128)(2,1)S(1)} %get-tuple-element.14), channel_id=1, source_target_pairs={{0,6},{1,7},{2,0},{3,1},{4,2},{5,3},{6,4},{7,5},{8,14},{9,15},{10,... | collective-permute-start | bytes 393224 | tf_op jit(solution)/shard_map/ppermute | solution.py:273
  65.4 0.0 collective-permute-start.5
  65.4 0.0 collective-permute-done.refs_1_
  65.4 5.8 %collective-permute-start.6 = (bf16[512,128]{1,0:T(8,128)(2,1)S(1)}, bf16[512,128]{1,0:T(8,128)(2,1)S(1)}, u32[]{:S(2)}, u32[]{:S(2)}) collective-permute-start(bf16[512,128]{1,0:T(8,128)(2,1)S(1)} %get-tuple-element.16), channel_id=1, source_target_pairs={{0,7},{1,6},{2,1},{3,0},{4,3},{5,2},{6,5},{7,4},{8,15},{9,14},{10,... | collective-permute-start | bytes 393224 | tf_op jit(solution)/shard_map/ppermute | solution.py:273
  71.2 0.0 collective-permute-done.3.refs_4_
  71.2 0.1 collective-permute-start.4
  71.3 0.0 collective-permute-done.1.refs_2_
  71.3 0.0 collective-permute-done.2.refs_3_
  71.3 1.4 %collective-permute-done.5.refs_6_ = bf16[512,128]{1,0:T(8,128)(2,1)S(1)} collective-permute-done((bf16[512,128]{1,0:T(8,128)(2,1)S(1)}, bf16[512,128]{1,0:T(8,128)(2,1)S(1)}, u32[]{:S(2)}, u32[]{:S(2)}) %collective-permute-start.5) | collective-permute-done | bytes 131104 | tf_op jit(solution)/shard_map/ppermute | solution.py:273
  72.7 0.7 collective-permute-done.6.refs_7_
  73.4 0.0 collective-permute-done.4.refs_5_
  73.4 0.0 copy-done.1
  73.4 3.5 %solve.1 = f32[64,64,128]{2,1,0:T(8,128)} custom-call(s32[512]{0:T(512)S(1)} %copy-done.2, bf16[64,128,128]{2,1,0:T(8,128)(2,1)S(1)} %copy-done.1, bf16[2,512,128]{2,1,0:T(8,128)(2,1)S(1)} %get-tuple-element.11.refs_0_, bf16[2,512,128]{2,1,0:T(8,128)(2,1)S(1)} %collective-permute-done.refs_1_, bf16[512,128]{1,0:T(8,128)(2,1)S(1)} %collective-permute-done.1.refs_2_, ...), custom_call_target="tpu_custom_call" | custom-call | tf_op jit(solution)/shard_map/solve/pallas_call | solution.py:254
  (2 shorter events, 0.0 us)
Async XLA Ops:
  0.0 0.7 copy-start.2
  0.7 53.0 %copy-start = (bf16[16,384,512]{2,1,0:T(8,128)(2,1)S(1)}, bf16[16,384,512]{2,1,0:T(8,128)(2,1)}, u32[]{:S(2)}) copy-start(bf16[16,384,512]{2,1,0:T(8,128)(2,1)} %table_ref.1) | copy-start | bytes 18874372
  53.7 19.7 %copy-start.1 = (bf16[64,128,128]{2,1,0:T(8,128)(2,1)S(1)}, bf16[64,128,128]{2,1,0:T(8,128)(2,1)}, u32[]{:S(2)}) copy-start(bf16[64,128,128]{2,1,0:T(8,128)(2,1)} %inverse_ref.1) | copy-start | bytes 6291460
  55.9 9.5 %collective-permute-start = (bf16[2,512,128]{2,1,0:T(8,128)(2,1)S(1)}, bf16[2,512,128]{2,1,0:T(8,128)(2,1)S(1)}, u32[]{:S(2)}, u32[]{:S(2)}) collective-permute-start(bf16[2,512,128]{2,1,0:T(8,128)(2,1)S(1)} %get-tuple-element.12), channel_id=1, source_target_pairs={{0,4},{1,5},{2,6},{3,7},{4,0},{5,1},{6,2},{7,3},{8,12},{9,13},{10,... | collective-permute-start | bytes 786440 | tf_op jit(solution)/shard_map/ppermute | solution.py:273
  58.7 12.5 %collective-permute-start.3 = (bf16[512,128]{1,0:T(8,128)(2,1)S(1)}, bf16[512,128]{1,0:T(8,128)(2,1)S(1)}, u32[]{:S(2)}, u32[]{:S(2)}) collective-permute-start(bf16[512,128]{1,0:T(8,128)(2,1)S(1)} %slice_bitcast_fusion.1), channel_id=1, source_target_pairs={{0,1},{1,0},{2,3},{3,2},{4,5},{5,4},{6,7},{7,6},{8,9},{9,8},{10,11... | collective-permute-start | bytes 393224 | tf_op jit(solution)/shard_map/ppermute | solution.py:273
  62.7 8.6 %collective-permute-start.1 = (bf16[512,128]{1,0:T(8,128)(2,1)S(1)}, bf16[512,128]{1,0:T(8,128)(2,1)S(1)}, u32[]{:S(2)}, u32[]{:S(2)}) collective-permute-start(bf16[512,128]{1,0:T(8,128)(2,1)S(1)} %get-tuple-element.13), channel_id=1, source_target_pairs={{0,2},{1,3},{2,4},{3,5},{4,6},{5,7},{6,0},{7,1},{8,10},{9,11},{10,... | collective-permute-start | bytes 393224 | tf_op jit(solution)/shard_map/ppermute | solution.py:273
  63.0 8.3 %collective-permute-start.2 = (bf16[512,128]{1,0:T(8,128)(2,1)S(1)}, bf16[512,128]{1,0:T(8,128)(2,1)S(1)}, u32[]{:S(2)}, u32[]{:S(2)}) collective-permute-start(bf16[512,128]{1,0:T(8,128)(2,1)S(1)} %get-tuple-element.14), channel_id=1, source_target_pairs={{0,6},{1,7},{2,0},{3,1},{4,2},{5,3},{6,4},{7,5},{8,14},{9,15},{10,... | collective-permute-start | bytes 393224 | tf_op jit(solution)/shard_map/ppermute | solution.py:273
  65.4 7.3 %collective-permute-start.5 = (bf16[512,128]{1,0:T(8,128)(2,1)S(1)}, bf16[512,128]{1,0:T(8,128)(2,1)S(1)}, u32[]{:S(2)}, u32[]{:S(2)}) collective-permute-start(bf16[512,128]{1,0:T(8,128)(2,1)S(1)} %get-tuple-element.15), channel_id=1, source_target_pairs={{0,3},{1,2},{2,5},{3,4},{4,7},{5,6},{6,1},{7,0},{8,11},{9,10},{10,... | collective-permute-start | bytes 393224 | tf_op jit(solution)/shard_map/ppermute | solution.py:273
  65.4 8.0 %collective-permute-start.6 = (bf16[512,128]{1,0:T(8,128)(2,1)S(1)}, bf16[512,128]{1,0:T(8,128)(2,1)S(1)}, u32[]{:S(2)}, u32[]{:S(2)}) collective-permute-start(bf16[512,128]{1,0:T(8,128)(2,1)S(1)} %get-tuple-element.16), channel_id=1, source_target_pairs={{0,7},{1,6},{2,1},{3,0},{4,3},{5,2},{6,5},{7,4},{8,15},{9,14},{10,... | collective-permute-start | bytes 393224 | tf_op jit(solution)/shard_map/ppermute | solution.py:273
  71.2 2.2 %collective-permute-start.4 = (bf16[512,128]{1,0:T(8,128)(2,1)S(1)}, bf16[512,128]{1,0:T(8,128)(2,1)S(1)}, u32[]{:S(2)}, u32[]{:S(2)}) collective-permute-start(bf16[512,128]{1,0:T(8,128)(2,1)S(1)} %slice_bitcast_fusion), channel_id=1, source_target_pairs={{0,1},{1,0},{2,3},{3,2},{4,5},{5,4},{6,7},{7,6},{8,9},{9,8},{10,11... | collective-permute-start | bytes 393224 | tf_op jit(solution)/shard_map/ppermute | solution.py:273

commit v6 on v5

--- a/solution.py
+++ b/solution.py
@@ -83,7 +83,7 @@
     for index in range(2):
         result = jnp.dot(mixed[index], table_ref[1, index], preferred_element_type=F32)
         for part in range(2):
-            high[index * 2 + part] = result[:, part * 128 : part * 128 + 128]
+            high[index * 2 + part, : columns * lats, :] = result[:, part * 128 : part * 128 + 128]
         for row in range(index * share, (index + 1) * share):
             turn(0, low, row)
 
@@ -120,9 +120,9 @@
             pltpu.VMEM(rows.shape, BF16),
             pltpu.VMEM(table.shape, BF16),
             pltpu.VMEM((2, count, HALF_LONS), BF16),
-            pltpu.VMEM((4, count, 128), F32),
-            pltpu.VMEM((4, count, 128), F32),
-            pltpu.VMEM((PAIRS * lats, 128), F32),
+            pltpu.VMEM((4, count + lats, 128), F32),
+            pltpu.VMEM((4, count + lats, 128), F32),
+            pltpu.VMEM((PAIRS * lats + lats, 128), F32),
             pltpu.SemaphoreType.DMA((8,)),
         ],
         compiler_params=pltpu.CompilerParams(vmem_limit_bytes=52 * 2**20),
@@ -258,7 +258,7 @@
         out_specs=HBM,
         scratch_shapes=[
             pltpu.VMEM((NR, lines * 8, 128), BF16),
-            pltpu.VMEM((lines * LINE, 128), F32),
+            pltpu.VMEM((lines * LINE + LINE, 128), F32),
             pltpu.VMEM((degrees // 8, lines, 8, 128), F32),
             pltpu.SemaphoreType.DMA((degrees // 8,)),
         ],

time: 77.2 us -> 77.2 us (level)
  no operation moved by 1% of the time
where the time goes in v6:
time: 77.2 us; the launch traced here: 76.9 us
  blocking collectives  48.5 us (63%)
  starting transfers between devices  15.4 us (20%)
  Pallas kernels  10.2 us (13%)
  waiting for transfers between devices  2.08 us (3%)
    all_to_all x1, blocking collectives, body(): received = lax.all_to_all(sent, 'ang', split_axis=0, concat_axis=0)  48.5 us
    ppermute x7, starting transfers between devices, move(): return lax.ppermute(part, 'rad', pairs)  15.4 us
    pallas_call x1, Pallas kernels, fourier_stage(): pl.pallas_call(functools.partial(fourier_kernel, lats), out_shape=jax.Sha...  4.54 us
    pallas_call x1, Pallas kernels, solve_stage(): pl.pallas_call(solve_kernel, out_shape=jax.ShapeDtypeStruct((lines, degre...  3.52 us
    pallas_call x1, Pallas kernels, legendre_stage(): pl.pallas_call(functools.partial(legendre_kernel, lats), out_shape=shapes...  2.11 us
    ppermute x7, waiting for transfers between devices, move(): return lax.ppermute(part, 'rad', pairs)  2.08 us
  transfers between devices with their start and end apart: 7, of which 2 were waited for; matrix products, arithmetic and copies ran while one was open for 0% of the time, Pallas kernels for 0%

profile of v6, /device:TPU:1, one launch (start us, length us, event | category | flops | bytes accessed | tf_op | source)
XLA Modules:
  0.0 76.9 jit_solution(2883797868447490009)
XLA Ops:
  0.0 0.0 copy-start.2
  0.0 0.7 copy-done.2
  0.7 0.0 copy-start
  0.7 4.5 %fourier.1 = bf16[32,192,128]{2,1,0:T(8,128)(2,1)S(1)} custom-call(s32[512]{0:T(512)S(1)} %copy-done.2, bf16[768,1536]{1,0:T(8,128)(2,1)} %bitcast.6, bf16[2,2,768,256]{3,2,1,0:T(8,128)(2,1)} %constant.2.clone.table_hbm), custom_call_target="tpu_custom_call" | custom-call | tf_op jit(solution)/shard_map/fourier/pallas_call | solution.py:113
  5.2 48.5 %all_to_all.5.received = bf16[32,192,128]{2,1,0:T(8,128)(2,1)S(1)} all-to-all(bf16[32,192,128]{2,1,0:T(8,128)(2,1)S(1)} %fourier.1), channel_id=1, replica_groups=mesh['ang'=32,'rad'=8] {'ang'}, dimensions={0} | all-to-all | bytes 3145728 | tf_op jit(solution)/shard_map/all_to_all | solution.py:292
  53.7 0.0 copy-done
  53.7 0.0 copy-start.1
  53.7 2.1 %legendre.1 = (bf16[2,512,128]{2,1,0:T(8,128)(2,1)S(1)}, bf16[512,128]{1,0:T(8,128)(2,1)S(1)}, bf16[512,128]{1,0:T(8,128)(2,1)S(1)}, bf16[2,512,128]{2,1,0:T(8,1...) custom-call(s32[512]{0:T(512)S(1)} %copy-done.2, bf16[16,384,512]{2,1,0:T(8,128)(2,1)S(1)} %copy-done, ...), custom_call_target="tpu_custom_call" | custom-call | tf_op jit(solution)/shard_map/legendre/pallas_call | solution.py:193
  55.8 2.8 %collective-permute-start = (bf16[2,512,128]{2,1,0:T(8,128)(2,1)S(1)}, bf16[2,512,128]{2,1,0:T(8,128)(2,1)S(1)}, u32[]{:S(2)}, u32[]{:S(2)}) collective-permute-start(bf16[2,512,128]{2,1,0:T(8,128)(2,1)S(1)} %get-tuple-element.12), channel_id=1, source_target_pairs={{0,4},{1,5},{2,6},{3,7},{4,0},{5,1},{6,2},{7,3},{8,12},{9,13},{10,... | collective-permute-start | bytes 786440 | tf_op jit(solution)/shard_map/ppermute | solution.py:273
  58.7 4.0 %collective-permute-start.3 = (bf16[512,128]{1,0:T(8,128)(2,1)S(1)}, bf16[512,128]{1,0:T(8,128)(2,1)S(1)}, u32[]{:S(2)}, u32[]{:S(2)}) collective-permute-start(bf16[512,128]{1,0:T(8,128)(2,1)S(1)} %slice_bitcast_fusion.1), channel_id=1, source_target_pairs={{0,1},{1,0},{2,3},{3,2},{4,5},{5,4},{6,7},{7,6},{8,9},{9,8},{10,11... | collective-permute-start | bytes 393224 | tf_op jit(solution)/shard_map/ppermute | solution.py:273
  62.7 0.3 collective-permute-start.1
  63.0 2.4 %collective-permute-start.2 = (bf16[512,128]{1,0:T(8,128)(2,1)S(1)}, bf16[512,128]{1,0:T(8,128)(2,1)S(1)}, u32[]{:S(2)}, u32[]{:S(2)}) collective-permute-start(bf16[512,128]{1,0:T(8,128)(2,1)S(1)} %get-tuple-element.14), channel_id=1, source_target_pairs={{0,6},{1,7},{2,0},{3,1},{4,2},{5,3},{6,4},{7,5},{8,14},{9,15},{10,... | collective-permute-start | bytes 393224 | tf_op jit(solution)/shard_map/ppermute | solution.py:273
  65.4 0.0 collective-permute-start.5
  65.4 0.0 collective-permute-done.refs_1_
  65.4 5.8 %collective-permute-start.6 = (bf16[512,128]{1,0:T(8,128)(2,1)S(1)}, bf16[512,128]{1,0:T(8,128)(2,1)S(1)}, u32[]{:S(2)}, u32[]{:S(2)}) collective-permute-start(bf16[512,128]{1,0:T(8,128)(2,1)S(1)} %get-tuple-element.16), channel_id=1, source_target_pairs={{0,7},{1,6},{2,1},{3,0},{4,3},{5,2},{6,5},{7,4},{8,15},{9,14},{10,... | collective-permute-start | bytes 393224 | tf_op jit(solution)/shard_map/ppermute | solution.py:273
  71.2 0.0 collective-permute-done.3.refs_4_
  71.2 0.1 collective-permute-start.4
  71.3 0.0 collective-permute-done.1.refs_2_
  71.3 0.0 collective-permute-done.2.refs_3_
  71.3 1.4 %collective-permute-done.5.refs_6_ = bf16[512,128]{1,0:T(8,128)(2,1)S(1)} collective-permute-done((bf16[512,128]{1,0:T(8,128)(2,1)S(1)}, bf16[512,128]{1,0:T(8,128)(2,1)S(1)}, u32[]{:S(2)}, u32[]{:S(2)}) %collective-permute-start.5) | collective-permute-done | bytes 131104 | tf_op jit(solution)/shard_map/ppermute | solution.py:273
  72.7 0.7 collective-permute-done.6.refs_7_
  73.4 0.0 collective-permute-done.4.refs_5_
  73.4 0.0 copy-done.1
  73.4 3.5 %solve.1 = f32[64,64,128]{2,1,0:T(8,128)} custom-call(s32[512]{0:T(512)S(1)} %copy-done.2, bf16[64,128,128]{2,1,0:T(8,128)(2,1)S(1)} %copy-done.1, bf16[2,512,128]{2,1,0:T(8,128)(2,1)S(1)} %get-tuple-element.11.refs_0_, bf16[2,512,128]{2,1,0:T(8,128)(2,1)S(1)} %collective-permute-done.refs_1_, bf16[512,128]{1,0:T(8,128)(2,1)S(1)} %collective-permute-done.1.refs_2_, ...), custom_call_target="tpu_custom_call" | custom-call | tf_op jit(solution)/shard_map/solve/pallas_call | solution.py:254
  (2 shorter events, 0.0 us)
Async XLA Ops:
  0.0 0.7 copy-start.2
  0.7 53.0 %copy-start = (bf16[16,384,512]{2,1,0:T(8,128)(2,1)S(1)}, bf16[16,384,512]{2,1,0:T(8,128)(2,1)}, u32[]{:S(2)}) copy-start(bf16[16,384,512]{2,1,0:T(8,128)(2,1)} %table_ref.1) | copy-start | bytes 18874372
  53.7 19.6 %copy-start.1 = (bf16[64,128,128]{2,1,0:T(8,128)(2,1)S(1)}, bf16[64,128,128]{2,1,0:T(8,128)(2,1)}, u32[]{:S(2)}) copy-start(bf16[64,128,128]{2,1,0:T(8,128)(2,1)} %inverse_ref.1) | copy-start | bytes 6291460
  55.8 9.5 %collective-permute-start = (bf16[2,512,128]{2,1,0:T(8,128)(2,1)S(1)}, bf16[2,512,128]{2,1,0:T(8,128)(2,1)S(1)}, u32[]{:S(2)}, u32[]{:S(2)}) collective-permute-start(bf16[2,512,128]{2,1,0:T(8,128)(2,1)S(1)} %get-tuple-element.12), channel_id=1, source_target_pairs={{0,4},{1,5},{2,6},{3,7},{4,0},{5,1},{6,2},{7,3},{8,12},{9,13},{10,... | collective-permute-start | bytes 786440 | tf_op jit(solution)/shard_map/ppermute | solution.py:273
  58.7 12.5 %collective-permute-start.3 = (bf16[512,128]{1,0:T(8,128)(2,1)S(1)}, bf16[512,128]{1,0:T(8,128)(2,1)S(1)}, u32[]{:S(2)}, u32[]{:S(2)}) collective-permute-start(bf16[512,128]{1,0:T(8,128)(2,1)S(1)} %slice_bitcast_fusion.1), channel_id=1, source_target_pairs={{0,1},{1,0},{2,3},{3,2},{4,5},{5,4},{6,7},{7,6},{8,9},{9,8},{10,11... | collective-permute-start | bytes 393224 | tf_op jit(solution)/shard_map/ppermute | solution.py:273
  62.7 8.6 %collective-permute-start.1 = (bf16[512,128]{1,0:T(8,128)(2,1)S(1)}, bf16[512,128]{1,0:T(8,128)(2,1)S(1)}, u32[]{:S(2)}, u32[]{:S(2)}) collective-permute-start(bf16[512,128]{1,0:T(8,128)(2,1)S(1)} %get-tuple-element.13), channel_id=1, source_target_pairs={{0,2},{1,3},{2,4},{3,5},{4,6},{5,7},{6,0},{7,1},{8,10},{9,11},{10,... | collective-permute-start | bytes 393224 | tf_op jit(solution)/shard_map/ppermute | solution.py:273
  63.0 8.3 %collective-permute-start.2 = (bf16[512,128]{1,0:T(8,128)(2,1)S(1)}, bf16[512,128]{1,0:T(8,128)(2,1)S(1)}, u32[]{:S(2)}, u32[]{:S(2)}) collective-permute-start(bf16[512,128]{1,0:T(8,128)(2,1)S(1)} %get-tuple-element.14), channel_id=1, source_target_pairs={{0,6},{1,7},{2,0},{3,1},{4,2},{5,3},{6,4},{7,5},{8,14},{9,15},{10,... | collective-permute-start | bytes 393224 | tf_op jit(solution)/shard_map/ppermute | solution.py:273
  65.4 7.3 %collective-permute-start.5 = (bf16[512,128]{1,0:T(8,128)(2,1)S(1)}, bf16[512,128]{1,0:T(8,128)(2,1)S(1)}, u32[]{:S(2)}, u32[]{:S(2)}) collective-permute-start(bf16[512,128]{1,0:T(8,128)(2,1)S(1)} %get-tuple-element.15), channel_id=1, source_target_pairs={{0,3},{1,2},{2,5},{3,4},{4,7},{5,6},{6,1},{7,0},{8,11},{9,10},{10,... | collective-permute-start | bytes 393224 | tf_op jit(solution)/shard_map/ppermute | solution.py:273
  65.4 8.0 %collective-permute-start.6 = (bf16[512,128]{1,0:T(8,128)(2,1)S(1)}, bf16[512,128]{1,0:T(8,128)(2,1)S(1)}, u32[]{:S(2)}, u32[]{:S(2)}) collective-permute-start(bf16[512,128]{1,0:T(8,128)(2,1)S(1)} %get-tuple-element.16), channel_id=1, source_target_pairs={{0,7},{1,6},{2,1},{3,0},{4,3},{5,2},{6,5},{7,4},{8,15},{9,14},{10,... | collective-permute-start | bytes 393224 | tf_op jit(solution)/shard_map/ppermute | solution.py:273
  71.2 2.2 %collective-permute-start.4 = (bf16[512,128]{1,0:T(8,128)(2,1)S(1)}, bf16[512,128]{1,0:T(8,128)(2,1)S(1)}, u32[]{:S(2)}, u32[]{:S(2)}) collective-permute-start(bf16[512,128]{1,0:T(8,128)(2,1)S(1)} %slice_bitcast_fusion), channel_id=1, source_target_pairs={{0,1},{1,0},{2,3},{3,2},{4,5},{5,4},{6,7},{7,6},{8,9},{9,8},{10,11... | collective-permute-start | bytes 393224 | tf_op jit(solution)/shard_map/ppermute | solution.py:273

commit v7 on v6

--- a/solution.py
+++ b/solution.py
@@ -104,7 +104,7 @@
             out_ref[device, local * lats : (local + 2) * lats, :] = jnp.concatenate(picked, axis=0).astype(BF16)
         return 0
 
-    lax.fori_loop(0, NA, put, 0, unroll=8)
+    lax.fori_loop(0, NA, put, 0, unroll=32)
 
 
 def fourier_stage(slot_order, rows, lats):

time: 77.2 us -> 77.1 us (level)
  no operation moved by 1% of the time
where the time goes in v7:
time: 77.1 us; the launch traced here: 76.9 us
  blocking collectives  48.5 us (63%)
  starting transfers between devices  15.4 us (20%)
  Pallas kernels  10.1 us (13%)
  waiting for transfers between devices  2.13 us (3%)
    all_to_all x1, blocking collectives, body(): received = lax.all_to_all(sent, 'ang', split_axis=0, concat_axis=0)  48.5 us
    ppermute x7, starting transfers between devices, move(): return lax.ppermute(part, 'rad', pairs)  15.4 us
    pallas_call x1, Pallas kernels, fourier_stage(): pl.pallas_call(functools.partial(fourier_kernel, lats), out_shape=jax.Sha...  4.45 us
    pallas_call x1, Pallas kernels, solve_stage(): pl.pallas_call(solve_kernel, out_shape=jax.ShapeDtypeStruct((lines, degre...  3.51 us
    ppermute x7, waiting for transfers between devices, move(): return lax.ppermute(part, 'rad', pairs)  2.13 us
    pallas_call x1, Pallas kernels, legendre_stage(): pl.pallas_call(functools.partial(legendre_kernel, lats), out_shape=shapes...  2.12 us
  transfers between devices with their start and end apart: 7, of which 2 were waited for; matrix products, arithmetic and copies ran while one was open for 0% of the time, Pallas kernels for 0%

profile of v7, /device:TPU:1, one launch (start us, length us, event | category | flops | bytes accessed | tf_op | source)
XLA Modules:
  0.0 76.9 jit_solution(11874653826266168926)
XLA Ops:
  0.0 0.0 copy-start.2
  0.0 0.7 copy-done.2
  0.7 0.0 copy-start
  0.7 4.5 %fourier.1 = bf16[32,192,128]{2,1,0:T(8,128)(2,1)S(1)} custom-call(s32[512]{0:T(512)S(1)} %copy-done.2, bf16[768,1536]{1,0:T(8,128)(2,1)} %bitcast.6, bf16[2,2,768,256]{3,2,1,0:T(8,128)(2,1)} %constant.2.clone.table_hbm), custom_call_target="tpu_custom_call" | custom-call | tf_op jit(solution)/shard_map/fourier/pallas_call | solution.py:113
  5.1 48.5 %all_to_all.5.received = bf16[32,192,128]{2,1,0:T(8,128)(2,1)S(1)} all-to-all(bf16[32,192,128]{2,1,0:T(8,128)(2,1)S(1)} %fourier.1), channel_id=1, replica_groups=mesh['ang'=32,'rad'=8] {'ang'}, dimensions={0} | all-to-all | bytes 3145728 | tf_op jit(solution)/shard_map/all_to_all | solution.py:292
  53.6 0.0 copy-done
  53.6 0.0 copy-start.1
  53.6 2.1 %legendre.1 = (bf16[2,512,128]{2,1,0:T(8,128)(2,1)S(1)}, bf16[512,128]{1,0:T(8,128)(2,1)S(1)}, bf16[512,128]{1,0:T(8,128)(2,1)S(1)}, bf16[2,512,128]{2,1,0:T(8,1...) custom-call(s32[512]{0:T(512)S(1)} %copy-done.2, bf16[16,384,512]{2,1,0:T(8,128)(2,1)S(1)} %copy-done, ...), custom_call_target="tpu_custom_call" | custom-call | tf_op jit(solution)/shard_map/legendre/pallas_call | solution.py:193
  55.8 2.8 %collective-permute-start = (bf16[2,512,128]{2,1,0:T(8,128)(2,1)S(1)}, bf16[2,512,128]{2,1,0:T(8,128)(2,1)S(1)}, u32[]{:S(2)}, u32[]{:S(2)}) collective-permute-start(bf16[2,512,128]{2,1,0:T(8,128)(2,1)S(1)} %get-tuple-element.12), channel_id=1, source_target_pairs={{0,4},{1,5},{2,6},{3,7},{4,0},{5,1},{6,2},{7,3},{8,12},{9,13},{10,... | collective-permute-start | bytes 786440 | tf_op jit(solution)/shard_map/ppermute | solution.py:273
  58.6 4.0 %collective-permute-start.3 = (bf16[512,128]{1,0:T(8,128)(2,1)S(1)}, bf16[512,128]{1,0:T(8,128)(2,1)S(1)}, u32[]{:S(2)}, u32[]{:S(2)}) collective-permute-start(bf16[512,128]{1,0:T(8,128)(2,1)S(1)} %slice_bitcast_fusion.1), channel_id=1, source_target_pairs={{0,1},{1,0},{2,3},{3,2},{4,5},{5,4},{6,7},{7,6},{8,9},{9,8},{10,11... | collective-permute-start | bytes 393224 | tf_op jit(solution)/shard_map/ppermute | solution.py:273
  62.6 0.3 collective-permute-start.1
  62.9 2.4 %collective-permute-start.2 = (bf16[512,128]{1,0:T(8,128)(2,1)S(1)}, bf16[512,128]{1,0:T(8,128)(2,1)S(1)}, u32[]{:S(2)}, u32[]{:S(2)}) collective-permute-start(bf16[512,128]{1,0:T(8,128)(2,1)S(1)} %get-tuple-element.14), channel_id=1, source_target_pairs={{0,6},{1,7},{2,0},{3,1},{4,2},{5,3},{6,4},{7,5},{8,14},{9,15},{10,... | collective-permute-start | bytes 393224 | tf_op jit(solution)/shard_map/ppermute | solution.py:273
  65.3 0.0 collective-permute-start.5
  65.3 0.0 collective-permute-done.refs_1_
  65.3 5.8 %collective-permute-start.6 = (bf16[512,128]{1,0:T(8,128)(2,1)S(1)}, bf16[512,128]{1,0:T(8,128)(2,1)S(1)}, u32[]{:S(2)}, u32[]{:S(2)}) collective-permute-start(bf16[512,128]{1,0:T(8,128)(2,1)S(1)} %get-tuple-element.16), channel_id=1, source_target_pairs={{0,7},{1,6},{2,1},{3,0},{4,3},{5,2},{6,5},{7,4},{8,15},{9,14},{10,... | collective-permute-start | bytes 393224 | tf_op jit(solution)/shard_map/ppermute | solution.py:273
  71.1 0.0 collective-permute-done.3.refs_4_
  71.1 0.1 collective-permute-start.4
  71.2 0.0 collective-permute-done.1.refs_2_
  71.2 0.0 collective-permute-done.2.refs_3_
  71.2 1.4 %collective-permute-done.5.refs_6_ = bf16[512,128]{1,0:T(8,128)(2,1)S(1)} collective-permute-done((bf16[512,128]{1,0:T(8,128)(2,1)S(1)}, bf16[512,128]{1,0:T(8,128)(2,1)S(1)}, u32[]{:S(2)}, u32[]{:S(2)}) %collective-permute-start.5) | collective-permute-done | bytes 131104 | tf_op jit(solution)/shard_map/ppermute | solution.py:273
  72.6 0.7 collective-permute-done.6.refs_7_
  73.3 0.0 collective-permute-done.4.refs_5_
  73.3 0.0 copy-done.1
  73.3 3.5 %solve.1 = f32[64,64,128]{2,1,0:T(8,128)} custom-call(s32[512]{0:T(512)S(1)} %copy-done.2, bf16[64,128,128]{2,1,0:T(8,128)(2,1)S(1)} %copy-done.1, bf16[2,512,128]{2,1,0:T(8,128)(2,1)S(1)} %get-tuple-element.11.refs_0_, bf16[2,512,128]{2,1,0:T(8,128)(2,1)S(1)} %collective-permute-done.refs_1_, bf16[512,128]{1,0:T(8,128)(2,1)S(1)} %collective-permute-done.1.refs_2_, ...), custom_call_target="tpu_custom_call" | custom-call | tf_op jit(solution)/shard_map/solve/pallas_call | solution.py:254
  (2 shorter events, 0.0 us)
Async XLA Ops:
  0.0 0.7 copy-start.2
  0.7 53.0 %copy-start = (bf16[16,384,512]{2,1,0:T(8,128)(2,1)S(1)}, bf16[16,384,512]{2,1,0:T(8,128)(2,1)}, u32[]{:S(2)}) copy-start(bf16[16,384,512]{2,1,0:T(8,128)(2,1)} %table_ref.1) | copy-start | bytes 18874372
  53.6 19.7 %copy-start.1 = (bf16[64,128,128]{2,1,0:T(8,128)(2,1)S(1)}, bf16[64,128,128]{2,1,0:T(8,128)(2,1)}, u32[]{:S(2)}) copy-start(bf16[64,128,128]{2,1,0:T(8,128)(2,1)} %inverse_ref.1) | copy-start | bytes 6291460
  55.8 9.5 %collective-permute-start = (bf16[2,512,128]{2,1,0:T(8,128)(2,1)S(1)}, bf16[2,512,128]{2,1,0:T(8,128)(2,1)S(1)}, u32[]{:S(2)}, u32[]{:S(2)}) collective-permute-start(bf16[2,512,128]{2,1,0:T(8,128)(2,1)S(1)} %get-tuple-element.12), channel_id=1, source_target_pairs={{0,4},{1,5},{2,6},{3,7},{4,0},{5,1},{6,2},{7,3},{8,12},{9,13},{10,... | collective-permute-start | bytes 786440 | tf_op jit(solution)/shard_map/ppermute | solution.py:273
  58.6 12.5 %collective-permute-start.3 = (bf16[512,128]{1,0:T(8,128)(2,1)S(1)}, bf16[512,128]{1,0:T(8,128)(2,1)S(1)}, u32[]{:S(2)}, u32[]{:S(2)}) collective-permute-start(bf16[512,128]{1,0:T(8,128)(2,1)S(1)} %slice_bitcast_fusion.1), channel_id=1, source_target_pairs={{0,1},{1,0},{2,3},{3,2},{4,5},{5,4},{6,7},{7,6},{8,9},{9,8},{10,11... | collective-permute-start | bytes 393224 | tf_op jit(solution)/shard_map/ppermute | solution.py:273
  62.6 8.6 %collective-permute-start.1 = (bf16[512,128]{1,0:T(8,128)(2,1)S(1)}, bf16[512,128]{1,0:T(8,128)(2,1)S(1)}, u32[]{:S(2)}, u32[]{:S(2)}) collective-permute-start(bf16[512,128]{1,0:T(8,128)(2,1)S(1)} %get-tuple-element.13), channel_id=1, source_target_pairs={{0,2},{1,3},{2,4},{3,5},{4,6},{5,7},{6,0},{7,1},{8,10},{9,11},{10,... | collective-permute-start | bytes 393224 | tf_op jit(solution)/shard_map/ppermute | solution.py:273
  62.9 8.3 %collective-permute-start.2 = (bf16[512,128]{1,0:T(8,128)(2,1)S(1)}, bf16[512,128]{1,0:T(8,128)(2,1)S(1)}, u32[]{:S(2)}, u32[]{:S(2)}) collective-permute-start(bf16[512,128]{1,0:T(8,128)(2,1)S(1)} %get-tuple-element.14), channel_id=1, source_target_pairs={{0,6},{1,7},{2,0},{3,1},{4,2},{5,3},{6,4},{7,5},{8,14},{9,15},{10,... | collective-permute-start | bytes 393224 | tf_op jit(solution)/shard_map/ppermute | solution.py:273
  65.3 7.3 %collective-permute-start.5 = (bf16[512,128]{1,0:T(8,128)(2,1)S(1)}, bf16[512,128]{1,0:T(8,128)(2,1)S(1)}, u32[]{:S(2)}, u32[]{:S(2)}) collective-permute-start(bf16[512,128]{1,0:T(8,128)(2,1)S(1)} %get-tuple-element.15), channel_id=1, source_target_pairs={{0,3},{1,2},{2,5},{3,4},{4,7},{5,6},{6,1},{7,0},{8,11},{9,10},{10,... | collective-permute-start | bytes 393224 | tf_op jit(solution)/shard_map/ppermute | solution.py:273
  65.3 8.0 %collective-permute-start.6 = (bf16[512,128]{1,0:T(8,128)(2,1)S(1)}, bf16[512,128]{1,0:T(8,128)(2,1)S(1)}, u32[]{:S(2)}, u32[]{:S(2)}) collective-permute-start(bf16[512,128]{1,0:T(8,128)(2,1)S(1)} %get-tuple-element.16), channel_id=1, source_target_pairs={{0,7},{1,6},{2,1},{3,0},{4,3},{5,2},{6,5},{7,4},{8,15},{9,14},{10,... | collective-permute-start | bytes 393224 | tf_op jit(solution)/shard_map/ppermute | solution.py:273
  71.1 2.2 %collective-permute-start.4 = (bf16[512,128]{1,0:T(8,128)(2,1)S(1)}, bf16[512,128]{1,0:T(8,128)(2,1)S(1)}, u32[]{:S(2)}, u32[]{:S(2)}) collective-permute-start(bf16[512,128]{1,0:T(8,128)(2,1)S(1)} %slice_bitcast_fusion), channel_id=1, source_target_pairs={{0,1},{1,0},{2,3},{3,2},{4,5},{5,4},{6,7},{7,6},{8,9},{9,8},{10,11... | collective-permute-start | bytes 393224 | tf_op jit(solution)/shard_map/ppermute | solution.py:273
